TPU v7x, 32 devices: a whole 2x2x4 slice. The times are simulated.
32 devices in a mesh: ens: 4 (over y, x), lat: 8 (over z, core).
Axes of the slice: x: 2, y: 2, z: 4, core: 2. Of those that a mesh axis runs over, the one named last changes fastest.
Arguments:
- features: bfloat16 [32, 128, 128], P('lat'), may hold values from -6 to 6
- random_perturbation: bfloat16 [4, 32, 128, 128], P('ens', 'lat'), may hold values from -6 to 6
- observed_truth: float32 [69, 32, 128], P(None, 'lat'), may hold values from -6 to 6
- stencil_taps: float32 [49, 128], replicated, may hold values from -0.875 to 0.875
- affine_factor: float32 [128], replicated, may hold values from 0.5 to 1.5
- widen_matrix: bfloat16 [512, 128], P('lat'), may hold values from -0.5 to 0.5
- shrink_matrix: bfloat16 [512, 128], P('lat'), may hold values from -0.25 to 0.25
- readout_matrix: bfloat16 [69, 128], replicated, may hold values from -0.5 to 0.5
Outputs:
- crps_score: float32 [], replicated
- stencil_taps_sensitivity: float32 [49, 128], replicated
- affine_factor_sensitivity: float32 [128], replicated
- widen_matrix_sensitivity: float32 [512, 128], P('lat')
- shrink_matrix_sensitivity: float32 [512, 128], P('lat')
- readout_matrix_sensitivity: float32 [69, 128], replicated
- sample_outlook: bfloat16 [4, 69, 32, 128], P('ens', None, 'lat')
- sample_average_spread: float32 [4, 69, 32, 128], P('ens', None, 'lat')
All inputs are finite; a program needn't handle non-finite values.
Results may differ from a plain program's by a relative error of at most 0.0024.
The roundings to bfloat16 on the way count: a program that leaves them out, or rounds other values in their place, can miss the bound.
Values may be sent and summed in bfloat16 or wider, within the bound.
A program may use at most 64 MiB of HBM per device.

v0:
```python
import math

import jax
import jax.numpy as jnp
from jax import lax
from jax.sharding import PartitionSpec as P

STENCIL_SIDE = 7


SQRT_TWO_PI = 0.7978845608028654
CUBIC = 0.044715
EPSILON = 1e-06
SMOOTHING = 0.01


def extended(cells, sides, width):
    for axis, dim in sides:
        count = lax.axis_size(axis)
        ends = count - 1
        head = lax.slice_in_dim(cells, 0, width, axis=dim)
        tail = lax.slice_in_dim(cells, cells.shape[dim] - width, cells.shape[dim], axis=dim)
        cells = jnp.concatenate(
            [
                lax.ppermute(tail, axis, [(i, (i + 1) % count) for i in range(ends)]),
                cells,
                lax.ppermute(head, axis, [((i + 1) % count, i) for i in range(ends)]),
            ],
            axis=dim,
        )
    return cells


def from_partner(value, axis, stride):
    return lax.ppermute(value, axis, [(i, i ^ 1 << stride) for i in range(lax.axis_size(axis))])


def smooth_magnitude(value):
    return jnp.sqrt(value * value + SMOOTHING)


def smooth_slope(value):
    return value * lax.rsqrt(value * value + SMOOTHING)


def gelu_tanh(northern_margin):
    return (
        0.5
        * northern_margin
        * (
            1.0
            + jnp.tanh(
                SQRT_TWO_PI
                * (northern_margin + CUBIC * northern_margin * northern_margin * northern_margin)
            )
        )
    )


def gelu_slope(northern_margin):
    inner = jnp.tanh(
        SQRT_TWO_PI
        * (northern_margin + CUBIC * northern_margin * northern_margin * northern_margin)
    )
    return 0.5 * (1.0 + inner) + 0.5 * northern_margin * (1.0 - inner * inner) * SQRT_TWO_PI * (
        1.0 + 3.0 * CUBIC * northern_margin * northern_margin
    )


def depthwise(margin_extended, stencil_taps, meridian_slab):
    half = STENCIL_SIDE // 2
    wide = margin_extended.astype(jnp.float32)
    axis_rows = wide.ndim - 3
    result = jnp.zeros(
        wide.shape[:axis_rows] + (meridian_slab,) + wide.shape[axis_rows + 1 :], jnp.float32
    )
    for offset_row in range(STENCIL_SIDE):
        band = lax.slice_in_dim(wide, offset_row, offset_row + meridian_slab, axis=axis_rows)
        for offset_col in range(STENCIL_SIDE):
            result = result + stencil_taps[offset_row * STENCIL_SIDE + offset_col] * jnp.roll(
                band, half - offset_col, axis=-2
            )
    return result


def kernel_grad(margin_extended, upstream, meridian_slab):
    half = STENCIL_SIDE // 2
    wide = margin_extended.astype(jnp.float32)
    axis_rows = wide.ndim - 3
    channels = upstream.shape[-1]
    taps = []
    for offset_row in range(STENCIL_SIDE):
        band = lax.slice_in_dim(wide, offset_row, offset_row + meridian_slab, axis=axis_rows)
        for offset_col in range(STENCIL_SIDE):
            shifted = jnp.roll(band, half - offset_col, axis=-2)
            taps.append(jnp.sum((upstream * shifted).reshape(-1, channels), axis=0))
    return jnp.stack(taps)


def normalize(depth_out):
    centre = jnp.mean(depth_out, axis=-1, keepdims=True)
    centred = depth_out - centre
    variance = jnp.mean(centred * centred, axis=-1, keepdims=True)
    reciprocal_spread = lax.rsqrt(variance + EPSILON)
    return (centred * reciprocal_spread, reciprocal_spread)


def pair_terms(carry, owned_subset, piece):

    def one_pair(totals, other):
        gap = owned_subset - other.astype(jnp.float32)[None]
        return ((totals[0] + smooth_magnitude(gap), totals[1] + smooth_slope(gap)), None)

    carry, ignored_entry = lax.scan(one_pair, carry, piece)
    return carry


def on_device(
    features,
    random_perturbation,
    observed_truth,
    stencil_taps,
    affine_factor,
    widen_matrix,
    shrink_matrix,
    readout_matrix,
):
    sample_count, meridian_slab, zonal_points, channels = random_perturbation.shape
    outlook_quantities = readout_matrix.shape[0]
    half = STENCIL_SIDE // 2
    latitudes = meridian_slab * lax.axis_size("lat")
    ensemble = sample_count * lax.axis_size("ens")
    point_tally = meridian_slab * zonal_points
    planar_map = (
        features[None].astype(jnp.float32) + random_perturbation.astype(jnp.float32)
    ).astype(jnp.bfloat16)
    margin_extended = extended(planar_map, (("lat", 1),), half)
    up_full, down_full = (
        lax.all_gather(widen_matrix, "lat", axis=0, tiled=True),
        lax.all_gather(shrink_matrix, "lat", axis=0, tiled=True),
    )
    depth_out = depthwise(margin_extended, stencil_taps, meridian_slab)
    factor_multiplied, reciprocal_spread = normalize(depth_out)
    standardized_activation = (
        (affine_factor * factor_multiplied)
        .astype(jnp.bfloat16)
        .reshape(sample_count * point_tally, channels)
    )
    northern_margin = lax.dot_general(
        standardized_activation,
        up_full,
        (((1,), (1,)), ((), ())),
        preferred_element_type=jnp.float32,
    )
    nonlinear_response = gelu_tanh(northern_margin).astype(jnp.bfloat16)
    mixed = jnp.dot(nonlinear_response, down_full, preferred_element_type=jnp.float32)
    skip_activation = (
        planar_map.reshape(sample_count * point_tally, channels).astype(jnp.float32) + mixed
    ).astype(jnp.bfloat16)
    residual_row_block = skip_activation.reshape(sample_count, point_tally, channels)
    sample_outlook = jnp.einsum(
        "au,blu->bal", readout_matrix, residual_row_block, preferred_element_type=jnp.float32
    )
    sample_outlook = sample_outlook.astype(jnp.bfloat16).reshape(
        sample_count, outlook_quantities, meridian_slab, zonal_points
    )
    row_index = (
        lax.axis_index("lat") * meridian_slab + jnp.arange(meridian_slab, dtype=jnp.int32)
    ).astype(jnp.float32)
    area = jnp.cos(math.pi * ((row_index + 0.5) / latitudes - 0.5))
    weight = (area * (1.0 / (latitudes * zonal_points)))[None, None, :, None]
    pair_norm = 1.0 / (ensemble * (ensemble - 1))
    owned_subset = sample_outlook.astype(jnp.float32)
    blank_buffer = jnp.zeros_like(owned_subset)
    spread, ranks = pair_terms((blank_buffer, blank_buffer), owned_subset, sample_outlook)
    held = sample_outlook
    for bit in range(lax.axis_size("ens").bit_length() - 1):
        other = from_partner(held, "ens", bit)
        spread, ranks = pair_terms((spread, ranks), owned_subset, other)
        held = jnp.concatenate([held, other], axis=0)
    miss = owned_subset - observed_truth[None]
    loss_part = jnp.sum(weight * (smooth_magnitude(miss) / ensemble - 0.5 * pair_norm * spread))
    carried_signal = (weight * (smooth_slope(miss) / ensemble - pair_norm * ranks)).astype(
        jnp.bfloat16
    )
    carried_signal = carried_signal.reshape(sample_count, outlook_quantities, point_tally)
    sample_average_spread = spread / (ensemble - 1)
    readout_matrix_sensitivity = jnp.einsum(
        "mvp,mpc->vc", carried_signal, residual_row_block, preferred_element_type=jnp.float32
    )
    back_residual = jnp.einsum(
        "mvp,vc->mpc", carried_signal, readout_matrix, preferred_element_type=jnp.float32
    )
    back_residual = back_residual.astype(jnp.bfloat16).reshape(sample_count * point_tally, channels)
    shrink_matrix_sensitivity = lax.dot_general(
        nonlinear_response,
        back_residual,
        (((0,), (0,)), ((), ())),
        preferred_element_type=jnp.float32,
    )
    back_gate = lax.dot_general(
        back_residual, down_full, (((1,), (1,)), ((), ())), preferred_element_type=jnp.float32
    )
    back_upper = (back_gate * gelu_slope(northern_margin)).astype(jnp.bfloat16)
    widen_matrix_sensitivity = lax.dot_general(
        back_upper,
        standardized_activation,
        (((0,), (0,)), ((), ())),
        preferred_element_type=jnp.float32,
    )
    back_norm = jnp.dot(back_upper, up_full, preferred_element_type=jnp.float32).reshape(
        sample_count, meridian_slab, zonal_points, channels
    )
    affine_factor_sensitivity = jnp.sum(
        (back_norm * factor_multiplied).reshape(-1, channels), axis=0
    )
    back_scaled = back_norm * affine_factor
    back_depth = reciprocal_spread * (
        back_scaled
        - jnp.mean(back_scaled, axis=-1, keepdims=True)
        - factor_multiplied * jnp.mean(back_scaled * factor_multiplied, axis=-1, keepdims=True)
    )
    stencil_taps_sensitivity = kernel_grad(margin_extended, back_depth, meridian_slab)
    summed_up, summed_down = lax.psum((widen_matrix_sensitivity, shrink_matrix_sensitivity), "ens")
    owned_up, owned_down = (
        lax.psum_scatter(summed_up, "lat", scatter_dimension=0, tiled=True),
        lax.psum_scatter(summed_down, "lat", scatter_dimension=0, tiled=True),
    )
    crps_score, total_out, total_gain, total_kernel = lax.psum(
        (
            loss_part,
            readout_matrix_sensitivity,
            affine_factor_sensitivity,
            stencil_taps_sensitivity,
        ),
        ("ens", "lat"),
    )
    return (
        crps_score,
        total_kernel,
        total_gain,
        owned_up,
        owned_down,
        total_out,
        sample_outlook,
        sample_average_spread,
    )


def solution(mesh):
    in_specs = (
        P("lat", None, None),
        P("ens", "lat", None, None),
        P(None, "lat", None),
        P(),
        P(),
        P("lat", None),
        P("lat", None),
        P(),
    )
    out_specs = (
        P(),
        P(),
        P(),
        P("lat", None),
        P("lat", None),
        P(),
        P("ens", None, "lat", None),
        P("ens", None, "lat", None),
    )
    return jax.shard_map(
        on_device, mesh=mesh, in_specs=in_specs, out_specs=out_specs, check_vma=False
    )
```

profile of v0, /device:TPU:0, one launch (start us, length us, event | category | flops | bytes accessed | tf_op | source)
XLA Modules:
  0.0 193.9 jit_solution(15689773625513776446)
XLA Ops:
  7.2 1.0 fusion.8
  8.3 2.4 %collective-permute-start = (bf16[1,3,128,128]{3,2,1,0:T(8,128)(2,1)S(1)}, bf16[1,3,128,128]{3,2,1,0:T(8,128)(2,1)S(1)}, u32[]{:S(2)}, u32[]{:S(2)}) collective-permute-start(bf16[1,3,128,128]{3,2,1,0:T(8,128)(2,1)S(1)} %get-tuple-element.235), channel_id=1, source_target_pairs={{0,1},{1,2},{2,3},{3,4},{4,5},{5,6},{6,7},{8,9},{9,10},{10,11},{11... | collective-permute-start | bytes 294920 | tf_op jit(solution)/shard_map/ppermute | solution.py:25
  10.7 1.3 collective-permute-start.1
  13.8 17.6 %all_gather.6 = bf16[512,128]{1,0:T(8,128)(2,1)S(1)} all-gather(bf16[64,128]{1,0:T(8,128)(2,1)S(1)} %copy-done.87), channel_id=1, replica_groups=mesh['ens'=4,'lat'=8] {'lat'}, dimensions={0}, use_global_device_ids=true | all-gather | bytes 147456 | tf_op jit(solution)/shard_map/all_gather | solution.py:139
  31.4 14.0 %all_gather.7 = bf16[512,128]{1,0:T(8,128)(2,1)S(1)} all-gather(bf16[64,128]{1,0:T(8,128)(2,1)S(1)} %copy-done.88), channel_id=1, replica_groups=mesh['ens'=4,'lat'=8] {'lat'}, dimensions={0}, use_global_device_ids=true | all-gather | bytes 147456 | tf_op jit(solution)/shard_map/all_gather | solution.py:140
  46.8 1.1 fusion.15
  48.0 1.3 maximum_convert_fusion.37
  54.6 3.8 %fusion.14 = (f32[4,128]{1,0:T(4,128)S(1)}, f32[1,4,128,128]{3,2,1,0:T(8,128)S(1)}) fusion(f32[1,4,3,128]{3,2,1,0:T(4,128)S(1)} %get-tuple-element.222, f32[1,4,125,128]{3,2,1,0:T(8,128)S(1)} %get-tuple-element.164, f32[128]{0:T(128)S(1)} %copy-done.133, f32[1,4,2,128]{3,2,1,0:T(2,128)} %get-tuple-element.194, ...), kind=kLoop, calls=%fused_computation.227 | loop fusion | flops 9174528 | bytes 13134336 | tf_op jit(solution)/shard_map/reduce_sum | solution.py:101
  59.9 1.4 multiply_convert_fusion
  62.7 1.5 collective-permute-start.2
  65.5 1.7 collective-permute-done.2
  67.8 1.5 collective-permute-start.3
  69.3 1.1 multiply_add_fusion.4
  70.5 2.5 %collective-permute-done.3 = bf16[2,69,4,128]{3,2,1,0:T(4,128)(2,1)S(1)} collective-permute-done((bf16[2,69,4,128]{3,2,1,0:T(4,128)(2,1)S(1)}, bf16[2,69,4,128]{3,2,1,0:T(4,128)(2,1)S(1)}, u32[]{:S(2)}, u32[]{:S(2)}) %collective-permute-start.3) | collective-permute-done | bytes 141344 | tf_op jit(solution)/shard_map/ppermute | solution.py:35
  73.6 2.2 %while.2 = (s32[]{:T(128)}, f32[1,69,4,128]{3,2,1,0:T(4,128)S(1)}, f32[1,69,4,128]{3,2,1,0:T(4,128)S(1)}, bf16[2,69,4,128]{3,2,1,0:T(4,128)(2,1)}, f32[1,69,4,128]{3,2,1,0:T(4,128)S(1)}, /*index=5*/s32[]{:T(128)}) while((s32[]{:T(128)}, f32[1,69,4,128]{3,2,1,0:T(4,128)S(1)}, f32[1,69,4,128]{3,2,1,0:T(4,128)S(1)}, ...), condition=%wide.region_3.4_spmd, body=%wide.region_2.3_spmd.sunk | while | flops 247298 | bytes 777289 | solution.py:114
  73.6 1.1 multiply_add_fusion.10
  74.7 1.1 multiply_add_fusion.10
  76.5 2.5 %fusion.13 = (bf16[69,4,128]{2,1,0:T(4,128)(2,1)S(1)}, f32[]{:T(128)}, f32[1,69,4,128]{3,2,1,0:T(4,128)}) fusion(f32[1,69,4,128]{3,2,1,0:T(4,128)S(1)} %get-tuple-element.67, f32[4]{0:T(128)S(1)} %copy-done.135, f32[69,4,128]{2,1,0:T(4,128)} %reshape.1627, f32[69,4,128]{2,1,0:T(4,128)} %param.12, f32[1,69,4,128]{3,2,1,0:T(4,128)S(1)} %get-tuple-element.66), kind=kLoop, calls=%fused_computation.135 | loop fusion | flops 529919 | bytes 777236
  79.3 1.0 fusion.21
  80.4 2.1 %fusion = bf16[512,512]{1,0:T(8,128)(2,1)S(1)} fusion(bf16[512,128]{1,0:T(8,128)(2,1)S(1)} %convolution_convert_fusion, bf16[512,128]{1,0:T(8,128)(2,1)} %copy-done.71, f32[512,512]{1,0:T(8,128)} %get-tuple-element.287), kind=kOutput, calls=%fused_computation.7 | convolution fusion | flops 72089600 | bytes 1835008 | tf_op jit(solution)/shard_map/dot_general | solution.py:201
  84.8 1.4 multiply_reduce_fusion.7
  86.4 1.2 multiply_reduce_fusion.17
  88.0 1.1 multiply_reduce_fusion.28
  89.1 1.1 fusion.20
  90.3 0.9 copy-done.2
  91.1 2.3 %multiply_reduce_fusion.38 = (f32[128]{0:T(128)}, f32[128]{0:T(128)}, f32[128]{0:T(128)}, f32[128]{0:T(128)}, f32[128]{0:T(128)}, /*index=5*/f32[128]{0:T(128)}, f32[128]{0:T(128)}, f32[128]{0:T(128)}, f32[128]{0:T(128)}) fusion(f32[1,4,128,128]{3,2,1,0:T(8,128)S(1)} %get-tuple-element.141, f32[1,4,1,128]{3,2,1,0:T(1,128)} %get-tuple-element.220, ...), kind=kLoop, calls=%fused_computation.102 | loop fusion | flops 1768320 | bytes 2626048 | tf_op jit(solution)/shard_map/reduce_sum | solution.py:96
  93.4 1.0 multiply_reduce_fusion.1
  94.6 17.2 %reduce-scatter.5.cloned.1.call-done = f32[64,128]{1,0:T(8,128)} async-done(((f32[512,128]{1,0:T(8,128)}), f32[64,128]{1,0:T(8,128)}) %reduce-scatter.5.cloned.1.call-update) | async-done | bytes 32784 | tf_op jit(solution)/shard_map/reduce_scatter | solution.py:227
  111.8 31.0 %reduce-scatter.3.cloned.1.call-done = f32[64,128]{1,0:T(8,128)} async-done(((f32[512,128]{1,0:T(8,128)}), f32[64,128]{1,0:T(8,128)}) %reduce-scatter.3.cloned.1.call-update) | async-done | bytes 32784 | tf_op jit(solution)/shard_map/reduce_scatter | solution.py:226
  143.8 39.4 %all-reduce = (f32[]{:T(128)}, f32[49,128]{1,0:T(8,128)}, f32[128]{0:T(128)}, f32[69,128]{1,0:T(8,128)}) all-reduce(f32[]{:T(128)} %get-tuple-element.231, f32[49,128]{1,0:T(8,128)S(1)} %stack.199, f32[128]{0:T(128)S(1)} %get-tuple-element.75, f32[69,128]{1,0:T(8,128)S(1)} %fusion.22), channel_id=1, replica_groups=mesh['ens'=4,'lat'=8] {'ens','lat'}, use_global_device_ids=true, to_apply=%region_5.6 | all-reduce | flops 15233 | bytes 121864 | tf_op jit(solution)/shard_map/psum | solution.py:229
  183.2 2.2 %all-reduce.4.cloned.1.call-done = (f32[64,128]{1,0:T(8,128)}, f32[64,128]{1,0:T(8,128)}) async-done(((f32[64,128]{1,0:T(8,128)}, f32[64,128]{1,0:T(8,128)}), (f32[64,128]{1,0:T(8,128)}, f32[64,128]{1,0:T(8,128)})) %all-reduce.4.cloned.1.call-update) | async-done | bytes 65552 | tf_op jit(solution)/shard_map/psum | solution.py:224
  185.4 1.4 copy.30
  (316 shorter events, 18.4 us)
Async XLA Ops:
  7.2 54.9 %copy-start = (bf16[69,128]{1,0:T(8,128)(2,1)S(1)}, bf16[69,128]{1,0:T(8,128)(2,1)}, u32[]{:S(2)}) copy-start(bf16[69,128]{1,0:T(8,128)(2,1)} %param.17) | copy-start | bytes 52996
  7.2 104.6 %reduce-scatter.5.cloned.1.call-start = ((), (), s32[]{:S(2)}) async-start(), calls=%async_computation.3 | async-start | bytes 294912 | tf_op jit(solution)/shard_map/reduce_scatter | solution.py:227
  8.3 37.1 %collective-permute-start = (bf16[1,3,128,128]{3,2,1,0:T(8,128)(2,1)S(1)}, bf16[1,3,128,128]{3,2,1,0:T(8,128)(2,1)S(1)}, u32[]{:S(2)}, u32[]{:S(2)}) collective-permute-start(bf16[1,3,128,128]{3,2,1,0:T(8,128)(2,1)S(1)} %get-tuple-element.235), channel_id=1, source_target_pairs={{0,1},{1,2},{2,3},{3,4},{4,5},{5,6},{6,7},{8,9},{9,10},{10,11},{11... | collective-permute-start | bytes 294920 | tf_op jit(solution)/shard_map/ppermute | solution.py:25
  10.7 34.8 %collective-permute-start.1 = (bf16[1,3,128,128]{3,2,1,0:T(8,128)(2,1)S(1)}, bf16[1,3,128,128]{3,2,1,0:T(8,128)(2,1)S(1)}, u32[]{:S(2)}, u32[]{:S(2)}) collective-permute-start(bf16[1,3,128,128]{3,2,1,0:T(8,128)(2,1)S(1)} %get-tuple-element.236), channel_id=1, source_target_pairs={{1,0},{2,1},{3,2},{4,3},{5,4},{6,5},{7,6},{9,8},{10,9},{11,10},{12... | collective-permute-start | bytes 294920 | tf_op jit(solution)/shard_map/ppermute | solution.py:27
  13.8 17.6 %copy-start.88 = (bf16[64,128]{1,0:T(8,128)(2,1)S(1)}, bf16[64,128]{1,0:T(8,128)(2,1)}, u32[]{:S(2)}) copy-start(bf16[64,128]{1,0:T(8,128)(2,1)} %param.16) | copy-start | bytes 49156
  31.4 28.4 %copy-start.69 = (bf16[512,128]{1,0:T(8,128)(2,1)}, bf16[512,128]{1,0:T(8,128)(2,1)S(1)}, u32[]{:S(2)}) copy-start(bf16[512,128]{1,0:T(8,128)(2,1)S(1)} %all_gather.6) | copy-start | bytes 393220
  45.4 15.9 %copy-start.71 = (bf16[512,128]{1,0:T(8,128)(2,1)}, bf16[512,128]{1,0:T(8,128)(2,1)S(1)}, u32[]{:S(2)}) copy-start(bf16[512,128]{1,0:T(8,128)(2,1)S(1)} %all_gather.7) | copy-start | bytes 393220
  45.8 8.1 %copy-start.9 = (f32[1,4,125,128]{3,2,1,0:T(8,128)}, f32[1,4,125,128]{3,2,1,0:T(8,128)S(1)}, u32[]{:S(2)}) copy-start(f32[1,4,125,128]{3,2,1,0:T(8,128)S(1)} %get-tuple-element.153) | copy-start | bytes 768004
  45.8 8.1 %copy-start.11 = (f32[1,4,125,128]{3,2,1,0:T(8,128)}, f32[1,4,125,128]{3,2,1,0:T(8,128)S(1)}, u32[]{:S(2)}) copy-start(f32[1,4,125,128]{3,2,1,0:T(8,128)S(1)} %get-tuple-element.154) | copy-start | bytes 768004
  45.8 8.1 %copy-start.13 = (f32[1,4,125,128]{3,2,1,0:T(8,128)}, f32[1,4,125,128]{3,2,1,0:T(8,128)S(1)}, u32[]{:S(2)}) copy-start(f32[1,4,125,128]{3,2,1,0:T(8,128)S(1)} %get-tuple-element.157) | copy-start | bytes 768004
  45.8 8.1 %copy-start.15 = (f32[1,4,125,128]{3,2,1,0:T(8,128)}, f32[1,4,125,128]{3,2,1,0:T(8,128)S(1)}, u32[]{:S(2)}) copy-start(f32[1,4,125,128]{3,2,1,0:T(8,128)S(1)} %get-tuple-element.158) | copy-start | bytes 768004
  45.8 8.1 %copy-start.27 = (f32[1,4,125,128]{3,2,1,0:T(8,128)}, f32[1,4,125,128]{3,2,1,0:T(8,128)S(1)}, u32[]{:S(2)}) copy-start(f32[1,4,125,128]{3,2,1,0:T(8,128)S(1)} %get-tuple-element.156) | copy-start | bytes 768004
  45.8 8.1 %copy-start.29 = (f32[1,4,125,128]{3,2,1,0:T(8,128)}, f32[1,4,125,128]{3,2,1,0:T(8,128)S(1)}, u32[]{:S(2)}) copy-start(f32[1,4,125,128]{3,2,1,0:T(8,128)S(1)} %get-tuple-element.159) | copy-start | bytes 768004
  45.8 8.1 %copy-start.45 = (f32[1,4,125,128]{3,2,1,0:T(8,128)}, f32[1,4,125,128]{3,2,1,0:T(8,128)S(1)}, u32[]{:S(2)}) copy-start(f32[1,4,125,128]{3,2,1,0:T(8,128)S(1)} %get-tuple-element.152) | copy-start | bytes 768004
  45.9 8.1 %copy-start.47 = (f32[1,4,125,128]{3,2,1,0:T(8,128)}, f32[1,4,125,128]{3,2,1,0:T(8,128)S(1)}, u32[]{:S(2)}) copy-start(f32[1,4,125,128]{3,2,1,0:T(8,128)S(1)} %get-tuple-element.155) | copy-start | bytes 768004
  45.9 8.1 %copy-start.49 = (f32[1,4,125,128]{3,2,1,0:T(8,128)}, f32[1,4,125,128]{3,2,1,0:T(8,128)S(1)}, u32[]{:S(2)}) copy-start(f32[1,4,125,128]{3,2,1,0:T(8,128)S(1)} %get-tuple-element.160) | copy-start | bytes 768004
  45.9 8.1 %copy-start.51 = (f32[1,4,125,128]{3,2,1,0:T(8,128)}, f32[1,4,125,128]{3,2,1,0:T(8,128)S(1)}, u32[]{:S(2)}) copy-start(f32[1,4,125,128]{3,2,1,0:T(8,128)S(1)} %get-tuple-element.163) | copy-start | bytes 768004
  46.2 7.7 %copy-start.1 = (f32[1,4,126,128]{3,2,1,0:T(8,128)}, f32[1,4,126,128]{3,2,1,0:T(8,128)S(1)}, u32[]{:S(2)}) copy-start(f32[1,4,126,128]{3,2,1,0:T(8,128)S(1)} %get-tuple-element.165) | copy-start | bytes 774148
  46.2 7.7 %copy-start.3 = (f32[1,4,126,128]{3,2,1,0:T(8,128)}, f32[1,4,126,128]{3,2,1,0:T(8,128)S(1)}, u32[]{:S(2)}) copy-start(f32[1,4,126,128]{3,2,1,0:T(8,128)S(1)} %get-tuple-element.175) | copy-start | bytes 774148
  46.3 7.7 %copy-start.4 = (f32[1,4,126,128]{3,2,1,0:T(8,128)}, f32[1,4,126,128]{3,2,1,0:T(8,128)S(1)}, u32[]{:S(2)}) copy-start(f32[1,4,126,128]{3,2,1,0:T(8,128)S(1)} %get-tuple-element.177) | copy-start | bytes 774148
  46.3 7.7 %copy-start.17 = (f32[1,4,126,128]{3,2,1,0:T(8,128)}, f32[1,4,126,128]{3,2,1,0:T(8,128)S(1)}, u32[]{:S(2)}) copy-start(f32[1,4,126,128]{3,2,1,0:T(8,128)S(1)} %get-tuple-element.171) | copy-start | bytes 774148
  46.3 7.7 %copy-start.19 = (f32[1,4,126,128]{3,2,1,0:T(8,128)}, f32[1,4,126,128]{3,2,1,0:T(8,128)S(1)}, u32[]{:S(2)}) copy-start(f32[1,4,126,128]{3,2,1,0:T(8,128)S(1)} %get-tuple-element.173) | copy-start | bytes 774148
  46.3 7.7 %copy-start.21 = (f32[1,4,126,128]{3,2,1,0:T(8,128)}, f32[1,4,126,128]{3,2,1,0:T(8,128)S(1)}, u32[]{:S(2)}) copy-start(f32[1,4,126,128]{3,2,1,0:T(8,128)S(1)} %get-tuple-element.174) | copy-start | bytes 774148
  46.3 7.7 %copy-start.31 = (f32[1,4,126,128]{3,2,1,0:T(8,128)}, f32[1,4,126,128]{3,2,1,0:T(8,128)S(1)}, u32[]{:S(2)}) copy-start(f32[1,4,126,128]{3,2,1,0:T(8,128)S(1)} %get-tuple-element.166) | copy-start | bytes 774148
  46.3 7.7 %copy-start.33 = (f32[1,4,126,128]{3,2,1,0:T(8,128)}, f32[1,4,126,128]{3,2,1,0:T(8,128)S(1)}, u32[]{:S(2)}) copy-start(f32[1,4,126,128]{3,2,1,0:T(8,128)S(1)} %get-tuple-element.169) | copy-start | bytes 774148
  46.3 7.7 %copy-start.35 = (f32[1,4,126,128]{3,2,1,0:T(8,128)}, f32[1,4,126,128]{3,2,1,0:T(8,128)S(1)}, u32[]{:S(2)}) copy-start(f32[1,4,126,128]{3,2,1,0:T(8,128)S(1)} %get-tuple-element.178) | copy-start | bytes 774148
  46.3 7.7 %copy-start.53 = (f32[1,4,126,128]{3,2,1,0:T(8,128)}, f32[1,4,126,128]{3,2,1,0:T(8,128)S(1)}, u32[]{:S(2)}) copy-start(f32[1,4,126,128]{3,2,1,0:T(8,128)S(1)} %get-tuple-element.167) | copy-start | bytes 774148
  46.3 7.7 %copy-start.55 = (f32[1,4,126,128]{3,2,1,0:T(8,128)}, f32[1,4,126,128]{3,2,1,0:T(8,128)S(1)}, u32[]{:S(2)}) copy-start(f32[1,4,126,128]{3,2,1,0:T(8,128)S(1)} %get-tuple-element.168) | copy-start | bytes 774148
  62.7 4.5 %collective-permute-start.2 = (bf16[1,69,4,128]{3,2,1,0:T(4,128)(2,1)S(1)}, bf16[1,69,4,128]{3,2,1,0:T(4,128)(2,1)S(1)}, u32[]{:S(2)}, u32[]{:S(2)}) collective-permute-start(bf16[1,69,4,128]{3,2,1,0:T(4,128)(2,1)S(1)} %reshape.1622), channel_id=1, source_target_pairs={{0,8},{8,0},{16,24},{24,16},{1,9},{9,1},{17,25},{25,17},{2,10},{10... | collective-permute-start | bytes 211976 | tf_op jit(solution)/shard_map/ppermute | solution.py:35
  67.8 5.2 %collective-permute-start.3 = (bf16[2,69,4,128]{3,2,1,0:T(4,128)(2,1)S(1)}, bf16[2,69,4,128]{3,2,1,0:T(4,128)(2,1)S(1)}, u32[]{:S(2)}, u32[]{:S(2)}) collective-permute-start(bf16[2,69,4,128]{3,2,1,0:T(4,128)(2,1)S(1)} %pad_maximum_fusion.42), channel_id=1, source_target_pairs={{0,16},{8,24},{16,0},{24,8},{1,17},{9,25},{17,1},{25,9},{2,18},{10... | collective-permute-start | bytes 423944 | tf_op jit(solution)/shard_map/ppermute | solution.py:35
  80.3 62.5 %reduce-scatter.3.cloned.1.call-start = ((), (), s32[]{:S(2)}) async-start(), calls=%async_computation.2 | async-start | bytes 294912 | tf_op jit(solution)/shard_map/reduce_scatter | solution.py:226
  90.2 95.2 %all-reduce.4.cloned.1.call-start = ((), (), s32[]{:S(2)}) async-start(), calls=%async_computation.4 | async-start | bytes 131072 | tf_op jit(solution)/shard_map/psum | solution.py:224
  (111 other events, 241.8 us)
Sparse Core Ops, SparseCore 0:
  80.4 31.3 reduce-scatter.4
  114.2 28.5 reduce-scatter.2
  145.7 39.6 all-reduce.3
where the time goes:
time: 195 us; the launch traced here: 194 us
  blocking collectives  70.9 us (36%)
  waiting for transfers between devices  54.6 us (28%)
  other arithmetic  24.8 us (13%)
  between operations  15.5 us (8%)
  local copies, waits for them, and re-layouts  14.4 us (7%)
  matrix products  6.84 us (4%)
  starting transfers between devices  6.79 us (3%)
    psum x1, blocking collectives, on_device(): lax.psum((loss_part, readout_matrix_sensitivity, affine_factor_sensitivit...  39.4 us
    reduce_scatter x1, waiting for transfers between devices, on_device(): lax.psum_scatter(summed_up, 'lat', scatter_dimension=0, tiled=True)  31 us
    all_gather x1, blocking collectives, on_device(): lax.all_gather(widen_matrix, 'lat', axis=0, tiled=True)  17.6 us
    reduce_scatter x1, waiting for transfers between devices, on_device(): lax.psum_scatter(summed_down, 'lat', scatter_dimension=0, tiled=True)  17.2 us
    all_gather x1, blocking collectives, on_device(): lax.all_gather(shrink_matrix, 'lat', axis=0, tiled=True)  14 us
    unnamed x276, local copies, waits for them, and re-layouts  9.52 us
    reduce_sum x6, other arithmetic, kernel_grad(): taps.append(jnp.sum((upstream * shifted).reshape(-1, channels), axis=0))  7.06 us
    slice x8, other arithmetic, depthwise(): jnp.roll(band, half - offset_col, axis=-2)  5.61 us
  transfers between devices with their start and end apart: 7, of which 5 were waited for; matrix products, arithmetic and copies ran while one was open for 8% of the time, Pallas kernels for 0%

commit v1 on v0

v1 whole, which is shorter than its diff:
```python
import functools
import math

import jax
import jax.numpy as jnp
from jax import lax
from jax.experimental import pallas as pl
from jax.experimental.pallas import tpu as pltpu
from jax.sharding import PartitionSpec as P

SIDE = 7
HALF = SIDE // 2
SQRT_TWO_PI = 0.7978845608028654
CUBIC = 0.044715
EPSILON = 1e-06
SMOOTHING = 0.01
PAD = 8
GRAD_ROW = 72
SMALL_ROWS = 128
F32 = jnp.float32
BF16 = jnp.bfloat16


def dot(a, b, dims):
    return lax.dot_general(a, b, (dims, ((), ())), preferred_element_type=F32)


def kernel(
    sizes,
    feat, noise, obs, taps, gain, widen, shrink, readout,
    crps_o, taps_o, gain_o, up_o, down_o, out_o, look_o, spread_o,
    ext, wide, tapb, depth, scaled_s, inv_s, normed, upper, inner, gated, ro, looks, wbuf,
    grads, rec_a, part_b, rec_b, part_c, rec_c, rec_d,
    small, small_a, small_pb, small_b, small_pc, small_c, small_d,
    halo_send, halo_recv, w_send, w_fwd, w_recv, e_send, e_recv,
    a_send, a_recv, b_send, b_recv, c_send, c_recv, d_send, d_recv,
):
    E, L = sizes
    Z = L // 2
    slab, zonal, channels = feat.shape
    quantities = obs.shape[0]
    rows = ro.shape[0]
    points = slab * zonal
    hidden = L * widen.shape[0]
    piece = widen.shape[0] // E
    ens = lax.axis_index("ens")
    lat = lax.axis_index("lat")
    z = lat // 2
    core = lat % 2
    sibling = z * 2 + (1 - core)

    def at(e, l):
        return {"ens": e, "lat": l}

    def remote(src, dst, send, recv, where):
        return pltpu.make_async_remote_copy(
            src_ref=src, dst_ref=dst, send_sem=send, recv_sem=recv,
            device_id=where, device_id_type=pl.DeviceIdType.MESH,
        )

    barrier = pltpu.get_barrier_semaphore()
    for k in range(1, L):
        pl.semaphore_signal(barrier, inc=1, device_id=at(ens, (lat + k) % L),
                            device_id_type=pl.DeviceIdType.MESH)
    for k in range(1, E):
        pl.semaphore_signal(barrier, inc=1, device_id=at((ens + k) % E, lat),
                            device_id_type=pl.DeviceIdType.MESH)

    def widen_rows(start, count):
        block = ext[start : start + count].astype(F32)
        wide[start : start + count, PAD : PAD + zonal, :] = block
        wide[start : start + count, 0:PAD, :] = block[:, zonal - PAD :, :]
        wide[start : start + count, PAD + zonal :, :] = block[:, :PAD, :]

    field = (feat[...].astype(F32) + noise[0].astype(F32)).astype(BF16)
    ext[HALF : HALF + slab] = field
    wbuf[pl.ds(lat, 1), 0] = widen[...][None]
    wbuf[pl.ds(lat, 1), 1] = shrink[...][None]
    pl.semaphore_wait(barrier, L - 1 + E - 1)

    south = remote(ext.at[pl.ds(slab, HALF)], ext.at[pl.ds(0, HALF)],
                   halo_send.at[0], halo_recv.at[0], at(ens, jnp.minimum(lat + 1, L - 1)))
    north = remote(ext.at[pl.ds(HALF, HALF)], ext.at[pl.ds(HALF + slab, HALF)],
                   halo_send.at[1], halo_recv.at[1], at(ens, jnp.maximum(lat - 1, 0)))

    @pl.when(lat < L - 1)
    def _():
        south.start()

    @pl.when(lat > 0)
    def _():
        north.start()

    own = [
        remote(wbuf.at[lat], wbuf.at[lat], w_send.at[k], w_recv.at[lat],
               at(ens, ((z + k) % Z) * 2 + core))
        for k in range(1, Z)
    ]
    for copy in own:
        copy.start()
    forwards = [remote(wbuf.at[lat], wbuf.at[lat], w_fwd.at[0], w_recv.at[lat], at(ens, sibling))]
    forwards[0].start()

    widen_rows(HALF, slab)
    for t in range(SIDE * SIDE):
        tapb[t] = jnp.broadcast_to(taps[t : t + 1, :], (8, channels))
    ro[...] = jnp.zeros_like(ro)
    ro[0:quantities, :] = readout[...]

    step = 32

    def convolve(ext_rows, fresh):
        def body(t, carry):
            base = pl.multiple_of(t * step, step)
            sums = []
            for i in range(slab):
                if fresh:
                    sums.append(jnp.zeros((step // 8, 8, channels), F32))
                else:
                    sums.append(depth[i, pl.ds(base, step), :].reshape(step // 8, 8, channels))
            for b in range(SIDE):
                for r in ext_rows:
                    x = wide[r, pl.ds(base + PAD - HALF + b, step), :].reshape(
                        step // 8, 8, channels)
                    for i in range(slab):
                        a = r - i
                        if 0 <= a < SIDE:
                            sums[i] = sums[i] + tapb[a * SIDE + b] * x
            for i in range(slab):
                depth[i, pl.ds(base, step), :] = sums[i].reshape(step, channels)
            return carry

        lax.fori_loop(0, zonal // step, body, 0)

    convolve(range(HALF, HALF + slab), True)

    for k in range(1, Z):
        other = ((z + k) % Z) * 2 + core
        remote(wbuf.at[other], wbuf.at[other], w_send.at[k], w_recv.at[other],
               at(ens, other)).wait_recv()
        copy = remote(wbuf.at[other], wbuf.at[other], w_fwd.at[k], w_recv.at[other],
                      at(ens, sibling))
        copy.start()
        forwards.append(copy)

    @pl.when(lat > 0)
    def _():
        south.wait_recv()
        widen_rows(0, HALF)

    @pl.when(lat == 0)
    def _():
        wide[0:HALF] = jnp.zeros((HALF, zonal + 2 * PAD, channels), F32)

    @pl.when(lat < L - 1)
    def _():
        north.wait_recv()
        widen_rows(HALF + slab, HALF)

    @pl.when(lat == L - 1)
    def _():
        wide[HALF + slab :] = jnp.zeros((HALF, zonal + 2 * PAD, channels), F32)

    convolve([*range(HALF), *range(HALF + slab, 2 * HALF + slab)], False)

    for i in range(slab):
        d = depth[i]
        centred = d - jnp.mean(d, axis=-1, keepdims=True)
        inverse = lax.rsqrt(jnp.mean(centred * centred, axis=-1, keepdims=True) + EPSILON)
        scaled = centred * inverse
        scaled_s[i] = scaled
        inv_s[i] = jnp.broadcast_to(inverse, (zonal, channels))
        normed[i * zonal : (i + 1) * zonal, :] = (gain[...] * scaled).astype(BF16)

    for k in range(Z):
        other = ((z + k) % Z) * 2 + (1 - core)
        remote(wbuf.at[other], wbuf.at[other], w_fwd.at[k], w_recv.at[other],
               at(ens, sibling)).wait_recv()

    up = wbuf[:, 0].reshape(hidden, channels)
    down = wbuf[:, 1].reshape(hidden, channels)
    upper[...] = dot(normed[...], up, ((1,), (1,)))

    sub = 16

    def gelu_step(t, carry):
        span = pl.ds(pl.multiple_of(t * sub, sub), sub)
        u = upper[span, :]
        th = jnp.tanh(SQRT_TWO_PI * (u + CUBIC * u * u * u))
        inner[span, :] = th
        gated[span, :] = (0.5 * u * (1.0 + th)).astype(BF16)
        return carry

    lax.fori_loop(0, points // sub, gelu_step, 0)

    mixed = dot(gated[...], down, ((1,), (0,)))
    residual = (
        ext[HALF : HALF + slab].reshape(points, channels).astype(F32) + mixed
    ).astype(BF16)
    mine = dot(ro[...], residual, ((1,), (1,))).astype(BF16)
    looks[pl.ds(ens, 1)] = mine[None]

    shares = [
        remote(looks.at[ens], looks.at[ens], e_send.at[k], e_recv.at[ens], at((ens + k) % E, lat))
        for k in range(1, E)
    ]
    for copy in shares:
        copy.start()

    look_o[...] = mine[:quantities]
    mine = mine.astype(F32)

    def slope_step(t, carry):
        span = pl.ds(pl.multiple_of(t * sub, sub), sub)
        u = upper[span, :]
        th = inner[span, :]
        inner[span, :] = 0.5 * (1.0 + th) + 0.5 * u * (1.0 - th * th) * SQRT_TWO_PI * (
            1.0 + 3.0 * CUBIC * u * u
        )
        return carry

    lax.fori_loop(0, points // sub, slope_step, 0)

    members = E
    pair_norm = 1.0 / (members * (members - 1))
    latitudes = slab * L
    cell = lax.broadcasted_iota(jnp.int32, (8, points), 1) // zonal + lat * slab
    area = jnp.cos(math.pi * ((cell.astype(F32) + 0.5) / latitudes - 0.5))
    weight = (area * (1.0 / (latitudes * zonal)))[0:1]

    truth = jnp.concatenate([obs[:, i, :] for i in range(slab)], axis=1)
    truth = jnp.concatenate([truth, jnp.zeros((rows - quantities, points), F32)], axis=0)
    miss = mine - truth
    square = miss * miss + SMOOTHING
    root = lax.rsqrt(square)
    miss_size = square * root
    miss_slope = miss * root

    spread = jnp.full((rows, points), math.sqrt(SMOOTHING), F32)
    ranks = jnp.zeros((rows, points), F32)
    for k in range(1, E):
        other = (ens + k) % E
        remote(looks.at[other], looks.at[other], e_send.at[k], e_recv.at[other],
               at(other, lat)).wait_recv()
        gap = mine - looks[pl.ds(other, 1)][0].astype(F32)
        square = gap * gap + SMOOTHING
        root = lax.rsqrt(square)
        spread = spread + square * root
        ranks = ranks + gap * root
    spread_o[...] = spread[:quantities] * (1.0 / (members - 1))
    loss = weight * (miss_size / members - 0.5 * pair_norm * spread)
    loss = jnp.sum(jnp.sum(loss[:quantities], axis=0, keepdims=True), axis=1, keepdims=True)
    flow = (weight * (miss_slope / members - pair_norm * ranks)).astype(BF16)

    def stash(slot, value):
        for l in range(L):
            for e in range(E):
                begin = (l * E + e) * piece
                grads[slot, l % 2, e, l // 2] = value[begin : begin + piece]

    def start_a(slot):
        copy = remote(grads.at[slot, 1 - core], rec_a.at[slot], a_send.at[slot], a_recv.at[slot],
                      at(ens, sibling))
        copy.start()
        return [copy]

    def scatter(src, dst, send, recv, me, count, place):
        copies = [
            remote(src((me + k) % count), dst.at[me], send.at[k], recv.at[me],
                   place((me + k) % count))
            for k in range(1, count)
        ]
        for copy in copies:
            copy.start()
        return copies

    def arrive(dst, send, recv, me, count, place):
        for k in range(1, count):
            other = (me + k) % count
            remote(dst.at[other], dst.at[other], send.at[k], recv.at[other],
                   place(other)).wait_recv()

    def by_ens(e):
        return at(e, lat)

    def by_z(other):
        return at(ens, other * 2 + core)

    def start_b(slot):
        sent = remote(grads.at[slot, 1 - core], rec_a.at[slot], a_send.at[slot], a_recv.at[slot],
                      at(ens, sibling))
        sent.wait_recv()
        part_b[slot] = grads[slot, pl.ds(core, 1)][0] + rec_a[slot]
        rec_b[slot, pl.ds(ens, 1)] = part_b[slot, pl.ds(ens, 1)]
        return scatter(lambda e: part_b.at[slot, e], rec_b.at[slot], b_send.at[slot],
                       b_recv.at[slot], ens, E, by_ens)

    def start_c(slot):
        arrive(rec_b.at[slot], b_send.at[slot], b_recv.at[slot], ens, E, by_ens)
        total = rec_b[slot, 0]
        for e in range(1, E):
            total = total + rec_b[slot, e]
        part_c[slot] = total
        rec_c[slot, pl.ds(z, 1)] = part_c[slot, pl.ds(z, 1)]
        return scatter(lambda o: part_c.at[slot, o], rec_c.at[slot], c_send.at[slot],
                       c_recv.at[slot], z, Z, by_z)

    def start_d(slot):
        arrive(rec_c.at[slot], c_send.at[slot], c_recv.at[slot], z, Z, by_z)
        total = rec_c[slot, 0]
        for o in range(1, Z):
            total = total + rec_c[slot, o]
        rec_d[slot, pl.ds(ens, 1)] = total[None]
        return scatter(lambda e: rec_d.at[slot, ens], rec_d.at[slot], d_send.at[slot],
                       d_recv.at[slot], ens, E, by_ens)

    def finish(slot, out):
        arrive(rec_d.at[slot], d_send.at[slot], d_recv.at[slot], ens, E, by_ens)
        for e in range(E):
            out[e * piece : (e + 1) * piece, :] = rec_d[slot, e]

    sent = []
    back_residual = dot(flow, ro[...], ((0,), (0,))).astype(BF16)
    stash(0, dot(gated[...], back_residual, ((0,), (0,))))
    sent += start_a(0)

    upper[...] = dot(back_residual, down, ((1,), (1,)))

    def back_step(t, carry):
        span = pl.ds(pl.multiple_of(t * sub, sub), sub)
        gated[span, :] = (upper[span, :] * inner[span, :]).astype(BF16)
        return carry

    lax.fori_loop(0, points // sub, back_step, 0)
    stash(1, dot(gated[...], normed[...], ((0,), (0,))))
    sent += start_a(1)
    sent += start_b(0)

    out_grad = dot(flow, residual, ((1,), (0,)))
    chunk = SMALL_ROWS // E

    def put(row, value):
        done = 0
        count = value.shape[0]
        while done < count:
            block, offset = divmod(row + done, chunk)
            take = min(count - done, chunk - offset)
            small[block, offset : offset + take, :] = value[done : done + take]
            done += take

    put(0, out_grad[:GRAD_ROW])

    upper[:, 0:channels] = dot(gated[...], up, ((1,), (0,)))
    gain_sum = jnp.zeros((1, channels), F32)
    for i in range(slab):
        back_norm = upper[i * zonal : (i + 1) * zonal, 0:channels]
        scaled = scaled_s[i]
        gain_sum = gain_sum + jnp.sum(back_norm * scaled, axis=0, keepdims=True)
        g = back_norm * gain[...]
        depth[i] = inv_s[i] * (
            g
            - jnp.mean(g, axis=-1, keepdims=True)
            - scaled * jnp.mean(g * scaled, axis=-1, keepdims=True)
        )
    sent += start_b(1)

    lane = 16
    for b in range(SIDE):
        def body(t, sums):
            base = pl.multiple_of(t * lane, lane)
            sums = list(sums)
            g = [depth[i, pl.ds(base, lane), :] for i in range(slab)]
            for r in range(2 * HALF + slab):
                x = wide[r, pl.ds(base + PAD - HALF + b, lane), :]
                for i in range(slab):
                    a = r - i
                    if 0 <= a < SIDE:
                        sums[a] = sums[a] + g[i] * x
            return tuple(sums)

        sums = lax.fori_loop(
            0, zonal // lane, body, tuple(jnp.zeros((lane, channels), F32) for _ in range(SIDE))
        )
        for a in range(SIDE):
            put(GRAD_ROW + a * SIDE + b, jnp.sum(sums[a], axis=0, keepdims=True))
    tail = GRAD_ROW + SIDE * SIDE
    put(tail, gain_sum)
    put(tail + 1, jnp.broadcast_to(loss, (1, channels)))
    put(tail + 2, jnp.zeros((SMALL_ROWS - tail - 2, channels), F32))

    copy = remote(small, small_a, a_send.at[2], a_recv.at[2], at(ens, sibling))
    copy.start()
    sent.append(copy)
    sent += start_c(0)
    copy.wait_recv()
    small_pb[...] = small[...] + small_a[...]
    small_b[pl.ds(ens, 1)] = small_pb[pl.ds(ens, 1)]
    sent += scatter(lambda e: small_pb.at[e], small_b, b_send.at[2], b_recv.at[2], ens, E, by_ens)
    sent += start_c(1)
    sent += start_d(0)
    arrive(small_b, b_send.at[2], b_recv.at[2], ens, E, by_ens)
    total = small_b[0]
    for e in range(1, E):
        total = total + small_b[e]
    small_pc[...] = total
    small_c[pl.ds(z, 1)] = total[None]
    sent += scatter(lambda o: small_pc, small_c, c_send.at[2], c_recv.at[2], z, Z, by_z)
    sent += start_d(1)
    arrive(small_c, c_send.at[2], c_recv.at[2], z, Z, by_z)
    total = small_c[0]
    for o in range(1, Z):
        total = total + small_c[o]
    small_d[pl.ds(ens, 1)] = total[None]
    sent += scatter(lambda e: small_d.at[ens], small_d, d_send.at[2], d_recv.at[2], ens, E, by_ens)
    finish(0, down_o)
    finish(1, up_o)
    arrive(small_d, d_send.at[2], d_recv.at[2], ens, E, by_ens)
    final = small_d[...].reshape(SMALL_ROWS, channels)
    out_o[...] = final[:quantities]
    taps_o[...] = final[GRAD_ROW:tail]
    gain_o[...] = final[tail : tail + 1]
    crps_o[...] = final[tail + 1 : tail + 2, 0:1]

    for copy in own + forwards + shares + sent:
        copy.wait_send()

    @pl.when(lat < L - 1)
    def _():
        south.wait_send()

    @pl.when(lat > 0)
    def _():
        north.wait_send()


def on_device(
    features, random_perturbation, observed_truth, stencil_taps,
    affine_factor, widen_matrix, shrink_matrix, readout_matrix,
):
    E, L = lax.axis_size("ens"), lax.axis_size("lat")
    Z = L // 2
    _, slab, zonal, channels = random_perturbation.shape
    quantities = readout_matrix.shape[0]
    unit = widen_matrix.shape[0]
    hidden = unit * L
    piece = unit // E
    points = slab * zonal
    rows = -(-quantities // 16) * 16
    chunk = SMALL_ROWS // E
    vmem = pl.BlockSpec(memory_space=pltpu.VMEM)
    dma = pltpu.SemaphoreType.DMA
    out = jax.ShapeDtypeStruct
    crps, taps, gain, up, down, head, look, spread = pl.pallas_call(
        functools.partial(kernel, (E, L)),
        out_shape=[
            out((1, 1), F32),
            out((SIDE * SIDE, channels), F32),
            out((1, channels), F32),
            out((unit, channels), F32),
            out((unit, channels), F32),
            out((quantities, channels), F32),
            out((quantities, points), BF16),
            out((quantities, points), F32),
        ],
        in_specs=[vmem] * 8,
        out_specs=[vmem] * 8,
        scratch_shapes=[
            pltpu.VMEM((slab + 2 * HALF, zonal, channels), BF16),
            pltpu.VMEM((slab + 2 * HALF, zonal + 2 * PAD, channels), F32),
            pltpu.VMEM((SIDE * SIDE, 8, channels), F32),
            pltpu.VMEM((slab, zonal, channels), F32),
            pltpu.VMEM((slab, zonal, channels), F32),
            pltpu.VMEM((slab, zonal, channels), F32),
            pltpu.VMEM((points, channels), BF16),
            pltpu.VMEM((points, hidden), F32),
            pltpu.VMEM((points, hidden), F32),
            pltpu.VMEM((points, hidden), BF16),
            pltpu.VMEM((rows, channels), BF16),
            pltpu.VMEM((E, rows, points), BF16),
            pltpu.VMEM((L, 2, unit, channels), BF16),
            pltpu.VMEM((2, 2, E, Z, piece, channels), F32),
            pltpu.VMEM((2, E, Z, piece, channels), F32),
            pltpu.VMEM((2, E, Z, piece, channels), F32),
            pltpu.VMEM((2, E, Z, piece, channels), F32),
            pltpu.VMEM((2, Z, piece, channels), F32),
            pltpu.VMEM((2, Z, piece, channels), F32),
            pltpu.VMEM((2, E, piece, channels), F32),
            pltpu.VMEM((E, chunk, channels), F32),
            pltpu.VMEM((E, chunk, channels), F32),
            pltpu.VMEM((E, chunk, channels), F32),
            pltpu.VMEM((E, chunk, channels), F32),
            pltpu.VMEM((chunk, channels), F32),
            pltpu.VMEM((Z, chunk, channels), F32),
            pltpu.VMEM((E, chunk, channels), F32),
            dma((2,)), dma((2,)),
            dma((Z,)), dma((Z,)), dma((L,)),
            dma((E,)), dma((E,)),
            dma((3,)), dma((3,)),
            dma((3, E)), dma((3, E)),
            dma((3, Z)), dma((3, Z)),
            dma((3, E)), dma((3, E)),
        ],
        compiler_params=pltpu.CompilerParams(
            collective_id=0, has_side_effects=True, vmem_limit_bytes=40 * 1024 * 1024
        ),
        cost_estimate=pl.CostEstimate(
            flops=12 * points * channels * hidden, bytes_accessed=2_000_000, transcendentals=0
        ),
    )(
        features, random_perturbation, observed_truth, stencil_taps,
        affine_factor.reshape(1, channels), widen_matrix, shrink_matrix, readout_matrix,
    )
    grid = (1, quantities, slab, zonal)
    return (
        crps.reshape(()), taps, gain.reshape(channels), up, down, head,
        look.reshape(grid), spread.reshape(grid),
    )


def solution(mesh):
    in_specs = (
        P("lat", None, None),
        P("ens", "lat", None, None),
        P(None, "lat", None),
        P(),
        P(),
        P("lat", None),
        P("lat", None),
        P(),
    )
    out_specs = (
        P(),
        P(),
        P(),
        P("lat", None),
        P("lat", None),
        P(),
        P("ens", None, "lat", None),
        P("ens", None, "lat", None),
    )
    return jax.shard_map(
        on_device, mesh=mesh, in_specs=in_specs, out_specs=out_specs, check_vma=False
    )
```

time: 195 us -> 50.5 us (0.26)
  blocking collectives: 70.9 us -> 0 us
  waiting for transfers between devices: 54.6 us -> 0 us
  Pallas kernels: 0 us -> 37 us
  other arithmetic: 24.8 us -> 0 us
  between operations: 15.5 us -> 2.48 us
  matrix products: 6.84 us -> 0 us
  starting transfers between devices: 6.79 us -> 0 us
  local copies, waits for them, and re-layouts: 14.4 us -> 10.6 us
    reduce_scatter x2 -> x0, waiting for transfers between devices: 48.2 us -> none  [the longest x1 31 us: on_device(): lax.psum_scatter(summed_up, 'lat', scatter_dimension=0, tiled=True)]
    psum x1 -> x0, blocking collectives: 39.4 us -> none  [on_device(): lax.psum((loss_part, readout_matrix_sensitivity, affine_factor_sensitivit...]
    pallas_call x0 -> x1, Pallas kernels: none -> 37 us  [on_device(): pl.pallas_call(functools.partial(kernel, (E, L)), out_shape=[out((1, 1),...]
    all_gather x2 -> x0, blocking collectives: 31.6 us -> none  [the longest x1 17.6 us: on_device(): lax.all_gather(widen_matrix, 'lat', axis=0, tiled=True)]
    reduce_sum x9 -> x0, other arithmetic: 11.4 us -> none  [the longest x6 7.06 us: kernel_grad(): taps.append(jnp.sum((upstream * shifted).reshape(-1, channels), axis=0))]
    dot_general x9 -> x0, matrix products: 6.84 us -> none  [the longest x1 2.12 us: on_device(): lax.dot_general(back_residual, down_full, (((1,), (1,)), ((), ())), prefe...]
    ppermute x4 -> x0, starting transfers between devices: 6.67 us -> none  [the longest x2 3.01 us: from_partner(): lax.ppermute(value, axis, [(i, i ^ 1 << stride) for i in range(lax.axis_s...]
    slice x8 -> x0, other arithmetic: 5.61 us -> none  [depthwise(): jnp.roll(band, half - offset_col, axis=-2)]
  transfers between devices with their start and end apart: 7 -> 0, of which waited for: 5 -> 0; matrix products, arithmetic and copies ran while one was open for 8% -> 0% of each run, Pallas kernels for 0% -> 0%
where the time goes in v1:
time: 50.5 us; the launch traced here: 50.1 us
  Pallas kernels  37 us (73%)
  local copies, waits for them, and re-layouts  10.6 us (21%)
  between operations  2.48 us (5%)
    pallas_call x1, Pallas kernels, on_device(): pl.pallas_call(functools.partial(kernel, (E, L)), out_shape=[out((1, 1),...  37 us
    unnamed x21, local copies, waits for them, and re-layouts  9.23 us

profile of v1, /device:TPU:0, one launch (start us, length us, event | category | flops | bytes accessed | tf_op | source)
XLA Modules:
  0.0 50.1 jit_solution(8116445227368312627)
XLA Ops:
  0.6 0.0 copy-start.7
  0.6 0.6 %copy-done.7 = f32[128]{0:T(128)S(1)} copy-done((f32[128]{0:T(128)S(1)}, f32[128]{0:T(128)}, u32[]{:S(2)}) %copy-start.7) | copy-done | bytes 536
  1.3 0.0 copy-start
  1.3 0.9 %copy-done = f32[69,4,128]{2,1,0:T(4,128)S(1)} copy-done((f32[69,4,128]{2,1,0:T(4,128)S(1)}, f32[69,4,128]{2,1,0:T(4,128)}, u32[]{:S(2)}) %copy-start) | copy-done | bytes 141336
  2.2 0.0 copy-start.1
  2.2 0.9 %copy-done.1 = bf16[4,128,128]{2,1,0:T(8,128)(2,1)S(1)} copy-done((bf16[4,128,128]{2,1,0:T(8,128)(2,1)S(1)}, bf16[4,128,128]{2,1,0:T(8,128)(2,1)}, u32[]{:S(2)}) %copy-start.1) | copy-done | bytes 131096
  3.1 0.0 copy-start.2
  3.1 0.9 %copy-done.2 = bf16[1,4,128,128]{3,2,1,0:T(8,128)(2,1)S(1)} copy-done((bf16[1,4,128,128]{3,2,1,0:T(8,128)(2,1)S(1)}, bf16[1,4,128,128]{3,2,1,0:T(8,128)(2,1)}, u32[]{:S(2)}) %copy-start.2) | copy-done | bytes 131096
  4.0 0.0 copy-start.3
  4.0 0.7 %copy-done.3 = f32[49,128]{1,0:T(8,128)S(1)} copy-done((f32[49,128]{1,0:T(8,128)S(1)}, f32[49,128]{1,0:T(8,128)}, u32[]{:S(2)}) %copy-start.3) | copy-done | bytes 25112
  4.8 0.0 copy-start.4
  4.8 0.7 %copy-done.4 = bf16[69,128]{1,0:T(8,128)(2,1)S(1)} copy-done((bf16[69,128]{1,0:T(8,128)(2,1)S(1)}, bf16[69,128]{1,0:T(8,128)(2,1)}, u32[]{:S(2)}) %copy-start.4) | copy-done | bytes 17688
  5.5 0.0 copy-start.5
  5.5 0.7 %copy-done.5 = bf16[64,128]{1,0:T(8,128)(2,1)S(1)} copy-done((bf16[64,128]{1,0:T(8,128)(2,1)S(1)}, bf16[64,128]{1,0:T(8,128)(2,1)}, u32[]{:S(2)}) %copy-start.5) | copy-done | bytes 16408
  6.2 0.0 copy-start.6
  6.2 0.7 %copy-done.6 = bf16[64,128]{1,0:T(8,128)(2,1)S(1)} copy-done((bf16[64,128]{1,0:T(8,128)(2,1)S(1)}, bf16[64,128]{1,0:T(8,128)(2,1)}, u32[]{:S(2)}) %copy-start.6) | copy-done | bytes 16408
  6.9 37.0 %shard_map.143 = (f32[1,1]{1,0:T(1,128)}, f32[49,128]{1,0:T(8,128)S(1)}, f32[1,128]{1,0:T(1,128)S(1)}, f32[64,128]{1,0:T(8,128)S(1)}, f32[64,128]{1,0:T(8,128)S(...) custom-call(bf16[4,128,128]{2,1,0:T(8,128)(2,1)S(1)} %copy-done.1, ...), custom_call_target="tpu_custom_call" | custom-call | flops 402653184 | bytes 2000000 | tf_op jit(solution)/shard_map/pallas_call | solution.py:453
  43.9 0.7 %reshape.34 = bf16[1,69,4,128]{3,2,1,0:T(4,128)(2,1)} reshape(bf16[69,512]{1,0:T(8,128)(2,1)S(1)} %get-tuple-element.22) | data formatting | bytes 141312 | tf_op jit(solution)/shard_map/reshape | solution.py:516
  44.6 0.7 %reshape.35 = f32[1,69,4,128]{3,2,1,0:T(4,128)} reshape(f32[69,512]{1,0:T(8,128)S(1)} %get-tuple-element.23) | data formatting | bytes 282624 | tf_op jit(solution)/shard_map/reshape | solution.py:516
  46.0 0.6 %copy.23 = f32[49,128]{1,0:T(8,128)} copy(f32[49,128]{1,0:T(8,128)S(1)} %get-tuple-element.33) | data formatting | bytes 50176
  46.6 0.5 %copy.24 = f32[128]{0:T(128)} copy(f32[128]{0:T(128)S(1)} %bitcast.4) | data formatting | bytes 1024
  47.1 0.6 %copy.25 = f32[64,128]{1,0:T(8,128)} copy(f32[64,128]{1,0:T(8,128)S(1)} %get-tuple-element.35) | data formatting | bytes 65536
  47.7 0.6 %copy.26 = f32[64,128]{1,0:T(8,128)} copy(f32[64,128]{1,0:T(8,128)S(1)} %get-tuple-element.36) | data formatting | bytes 65536
  48.3 0.6 %copy.27 = f32[69,128]{1,0:T(8,128)} copy(f32[69,128]{1,0:T(8,128)S(1)} %get-tuple-element.37) | data formatting | bytes 70656
Async XLA Ops:
  0.6 0.7 %copy-start.7 = (f32[128]{0:T(128)S(1)}, f32[128]{0:T(128)}, u32[]{:S(2)}) copy-start(f32[128]{0:T(128)} %param.12) | copy-start | bytes 1540
  1.3 0.9 %copy-start = (f32[69,4,128]{2,1,0:T(4,128)S(1)}, f32[69,4,128]{2,1,0:T(4,128)}, u32[]{:S(2)}) copy-start(f32[69,4,128]{2,1,0:T(4,128)} %obs.1) | copy-start | bytes 423940
  2.2 0.9 %copy-start.1 = (bf16[4,128,128]{2,1,0:T(8,128)(2,1)S(1)}, bf16[4,128,128]{2,1,0:T(8,128)(2,1)}, u32[]{:S(2)}) copy-start(bf16[4,128,128]{2,1,0:T(8,128)(2,1)} %feat.1) | copy-start | bytes 393220
  3.1 0.9 %copy-start.2 = (bf16[1,4,128,128]{3,2,1,0:T(8,128)(2,1)S(1)}, bf16[1,4,128,128]{3,2,1,0:T(8,128)(2,1)}, u32[]{:S(2)}) copy-start(bf16[1,4,128,128]{3,2,1,0:T(8,128)(2,1)} %noise.1) | copy-start | bytes 393220
  4.0 0.7 %copy-start.3 = (f32[49,128]{1,0:T(8,128)S(1)}, f32[49,128]{1,0:T(8,128)}, u32[]{:S(2)}) copy-start(f32[49,128]{1,0:T(8,128)} %taps.1) | copy-start | bytes 75268
  4.8 0.7 %copy-start.4 = (bf16[69,128]{1,0:T(8,128)(2,1)S(1)}, bf16[69,128]{1,0:T(8,128)(2,1)}, u32[]{:S(2)}) copy-start(bf16[69,128]{1,0:T(8,128)(2,1)} %readout.1) | copy-start | bytes 52996
  5.5 0.7 %copy-start.5 = (bf16[64,128]{1,0:T(8,128)(2,1)S(1)}, bf16[64,128]{1,0:T(8,128)(2,1)}, u32[]{:S(2)}) copy-start(bf16[64,128]{1,0:T(8,128)(2,1)} %widen.1) | copy-start | bytes 49156
  6.2 0.7 %copy-start.6 = (bf16[64,128]{1,0:T(8,128)(2,1)S(1)}, bf16[64,128]{1,0:T(8,128)(2,1)}, u32[]{:S(2)}) copy-start(bf16[64,128]{1,0:T(8,128)(2,1)} %shrink.1) | copy-start | bytes 49156

commit v2 on v1

--- a/solution.py
+++ b/solution.py
@@ -27,13 +27,16 @@
 
 def kernel(
     sizes,
-    feat, noise, obs, taps, gain, widen, shrink, readout,
+    feat_h, noise_h, obs_h, taps_h, gain_h, widen_h, shrink_h, readout_h,
     crps_o, taps_o, gain_o, up_o, down_o, out_o, look_o, spread_o,
+    feat, noise, obs, taps, gain, readout,
     ext, wide, tapb, depth, scaled_s, inv_s, normed, upper, inner, gated, ro, looks, wbuf,
+    resid, flows, back, gated_back, outlook, tap_grad,
     grads, rec_a, part_b, rec_b, part_c, rec_c, rec_d,
-    small, small_a, small_pb, small_b, small_pc, small_c, small_d,
-    halo_send, halo_recv, w_send, w_fwd, w_recv, e_send, e_recv,
+    small, small_b, small_pc, small_c, small_d,
+    in_sem, halo_send, halo_recv, w_send, w_fwd, w_recv, e_send, e_recv,
     a_send, a_recv, b_send, b_recv, c_send, c_recv, d_send, d_recv,
+    p_send, p_recv, q_send, q_recv, r_send, r_recv,
 ):
     E, L = sizes
     Z = L // 2
@@ -41,8 +44,8 @@
     quantities = obs.shape[0]
     rows = ro.shape[0]
     points = slab * zonal
-    hidden = L * widen.shape[0]
-    piece = widen.shape[0] // E
+    hidden = L * wbuf.shape[2]
+    piece = wbuf.shape[2] // E
     ens = lax.axis_index("ens")
     lat = lax.axis_index("lat")
     z = lat // 2
@@ -63,8 +66,20 @@
         pl.semaphore_signal(barrier, inc=1, device_id=at(ens, (lat + k) % L),
                             device_id_type=pl.DeviceIdType.MESH)
     for k in range(1, E):
-        pl.semaphore_signal(barrier, inc=1, device_id=at((ens + k) % E, lat),
-                            device_id_type=pl.DeviceIdType.MESH)
+        for l in (lat, sibling):
+            pl.semaphore_signal(barrier, inc=1, device_id=at((ens + k) % E, l),
+                                device_id_type=pl.DeviceIdType.MESH)
+
+    loads = [
+        pltpu.make_async_copy(src, dst, in_sem.at[n])
+        for n, (src, dst) in enumerate([
+            (feat_h, feat), (noise_h, noise), (widen_h, wbuf.at[lat, 0]),
+            (shrink_h, wbuf.at[lat, 1]), (taps_h, taps), (readout_h, readout),
+            (gain_h, gain), (obs_h, obs),
+        ])
+    ]
+    for copy in loads:
+        copy.start()
 
     def widen_rows(start, count):
         block = ext[start : start + count].astype(F32)
@@ -72,11 +87,11 @@
         wide[start : start + count, 0:PAD, :] = block[:, zonal - PAD :, :]
         wide[start : start + count, PAD + zonal :, :] = block[:, :PAD, :]
 
+    loads[0].wait()
+    loads[1].wait()
     field = (feat[...].astype(F32) + noise[0].astype(F32)).astype(BF16)
     ext[HALF : HALF + slab] = field
-    wbuf[pl.ds(lat, 1), 0] = widen[...][None]
-    wbuf[pl.ds(lat, 1), 1] = shrink[...][None]
-    pl.semaphore_wait(barrier, L - 1 + E - 1)
+    pl.semaphore_wait(barrier, L - 1 + 2 * (E - 1))
 
     south = remote(ext.at[pl.ds(slab, HALF)], ext.at[pl.ds(0, HALF)],
                    halo_send.at[0], halo_recv.at[0], at(ens, jnp.minimum(lat + 1, L - 1)))
@@ -96,12 +111,16 @@
                at(ens, ((z + k) % Z) * 2 + core))
         for k in range(1, Z)
     ]
+    loads[2].wait()
+    loads[3].wait()
     for copy in own:
         copy.start()
     forwards = [remote(wbuf.at[lat], wbuf.at[lat], w_fwd.at[0], w_recv.at[lat], at(ens, sibling))]
     forwards[0].start()
 
     widen_rows(HALF, slab)
+    for copy in loads[4:]:
+        copy.wait()
     for t in range(SIDE * SIDE):
         tapb[t] = jnp.broadcast_to(taps[t : t + 1, :], (8, channels))
     ro[...] = jnp.zeros_like(ro)
@@ -179,78 +198,77 @@
 
     up = wbuf[:, 0].reshape(hidden, channels)
     down = wbuf[:, 1].reshape(hidden, channels)
-    upper[...] = dot(normed[...], up, ((1,), (1,)))
-
-    sub = 16
-
-    def gelu_step(t, carry):
-        span = pl.ds(pl.multiple_of(t * sub, sub), sub)
-        u = upper[span, :]
-        th = jnp.tanh(SQRT_TWO_PI * (u + CUBIC * u * u * u))
-        inner[span, :] = th
-        gated[span, :] = (0.5 * u * (1.0 + th)).astype(BF16)
-        return carry
-
-    lax.fori_loop(0, points // sub, gelu_step, 0)
-
-    mixed = dot(gated[...], down, ((1,), (0,)))
-    residual = (
-        ext[HALF : HALF + slab].reshape(points, channels).astype(F32) + mixed
-    ).astype(BF16)
-    mine = dot(ro[...], residual, ((1,), (1,))).astype(BF16)
-    looks[pl.ds(ens, 1)] = mine[None]
-
-    shares = [
-        remote(looks.at[ens], looks.at[ens], e_send.at[k], e_recv.at[ens], at((ens + k) % E, lat))
-        for k in range(1, E)
-    ]
-    for copy in shares:
-        copy.start()
-
-    look_o[...] = mine[:quantities]
-    mine = mine.astype(F32)
-
-    def slope_step(t, carry):
-        span = pl.ds(pl.multiple_of(t * sub, sub), sub)
-        u = upper[span, :]
-        th = inner[span, :]
-        inner[span, :] = 0.5 * (1.0 + th) + 0.5 * u * (1.0 - th * th) * SQRT_TWO_PI * (
+    sub = 32
+    shares = []
+    for i in range(slab):
+        begin, end = i * zonal, (i + 1) * zonal
+        upper[begin:end, :] = dot(normed[begin:end, :], up, ((1,), (1,)))
+        for t in range(begin, end, sub):
+            u = upper[t : t + sub, :]
+            th = jnp.tanh(SQRT_TWO_PI * (u + CUBIC * u * u * u))
+            inner[t : t + sub, :] = th
+            gated[t : t + sub, :] = (0.5 * u * (1.0 + th)).astype(BF16)
+        mixed = dot(gated[begin:end, :], down, ((1,), (0,)))
+        residual = (ext[HALF + i].astype(F32) + mixed).astype(BF16)
+        resid[begin:end, :] = residual
+        mine = dot(ro[...], residual, ((1,), (1,))).astype(BF16)
+        looks[i, pl.ds(ens, 1)] = mine[None]
+        for k in range(1, E):
+            copy = remote(looks.at[i, ens], looks.at[i, ens], e_send.at[i, k], e_recv.at[i, ens],
+                          at((ens + k) % E, lat))
+            copy.start()
+            shares.append(copy)
+        outlook[:, i, :] = mine.astype(F32)
+
+    look_o[0] = outlook[0:quantities].astype(BF16)
+
+    for t in range(0, points, sub):
+        u = upper[t : t + sub, :]
+        th = inner[t : t + sub, :]
+        inner[t : t + sub, :] = 0.5 * (1.0 + th) + 0.5 * u * (1.0 - th * th) * SQRT_TWO_PI * (
             1.0 + 3.0 * CUBIC * u * u
         )
-        return carry
-
-    lax.fori_loop(0, points // sub, slope_step, 0)
 
     members = E
     pair_norm = 1.0 / (members * (members - 1))
     latitudes = slab * L
-    cell = lax.broadcasted_iota(jnp.int32, (8, points), 1) // zonal + lat * slab
-    area = jnp.cos(math.pi * ((cell.astype(F32) + 0.5) / latitudes - 0.5))
-    weight = (area * (1.0 / (latitudes * zonal)))[0:1]
-
-    truth = jnp.concatenate([obs[:, i, :] for i in range(slab)], axis=1)
-    truth = jnp.concatenate([truth, jnp.zeros((rows - quantities, points), F32)], axis=0)
-    miss = mine - truth
-    square = miss * miss + SMOOTHING
-    root = lax.rsqrt(square)
-    miss_size = square * root
-    miss_slope = miss * root
-
-    spread = jnp.full((rows, points), math.sqrt(SMOOTHING), F32)
-    ranks = jnp.zeros((rows, points), F32)
-    for k in range(1, E):
-        other = (ens + k) % E
-        remote(looks.at[other], looks.at[other], e_send.at[k], e_recv.at[other],
-               at(other, lat)).wait_recv()
-        gap = mine - looks[pl.ds(other, 1)][0].astype(F32)
-        square = gap * gap + SMOOTHING
+    loss = jnp.zeros((1, channels), F32)
+    for i in range(slab):
+        begin, end = i * zonal, (i + 1) * zonal
+        row = jnp.full((8, zonal), lat * slab + i, jnp.int32).astype(F32)
+        area = jnp.cos(math.pi * ((row + 0.5) / latitudes - 0.5))
+        weight = (area * (1.0 / (latitudes * zonal)))[0:1]
+        mine = looks[i, pl.ds(ens, 1)][0].astype(F32)
+        truth = jnp.concatenate(
+            [obs[:, i, :], jnp.zeros((rows - quantities, zonal), F32)], axis=0)
+        miss = mine - truth
+        square = miss * miss + SMOOTHING
         root = lax.rsqrt(square)
-        spread = spread + square * root
-        ranks = ranks + gap * root
-    spread_o[...] = spread[:quantities] * (1.0 / (members - 1))
-    loss = weight * (miss_size / members - 0.5 * pair_norm * spread)
-    loss = jnp.sum(jnp.sum(loss[:quantities], axis=0, keepdims=True), axis=1, keepdims=True)
-    flow = (weight * (miss_slope / members - pair_norm * ranks)).astype(BF16)
+        miss_size = square * root
+        miss_slope = miss * root
+        spread = jnp.full((rows, zonal), math.sqrt(SMOOTHING), F32)
+        ranks = jnp.zeros((rows, zonal), F32)
+        for k in range(1, E):
+            other = (ens + k) % E
+            remote(looks.at[i, other], looks.at[i, other], e_send.at[i, k], e_recv.at[i, other],
+                   at(other, lat)).wait_recv()
+            gap = mine - looks[i, pl.ds(other, 1)][0].astype(F32)
+            square = gap * gap + SMOOTHING
+            root = lax.rsqrt(square)
+            spread = spread + square * root
+            ranks = ranks + gap * root
+        spread_o[0, :, i, :] = spread[:quantities] * (1.0 / (members - 1))
+        part = weight * (miss_size / members - 0.5 * pair_norm * spread)
+        loss = loss + jnp.sum(part[:quantities], axis=0, keepdims=True)
+        flow = (weight * (miss_slope / members - pair_norm * ranks)).astype(BF16)
+        flows[:, begin:end] = flow
+        back_residual = dot(flow, ro[...], ((0,), (0,))).astype(BF16)
+        back[begin:end, :] = back_residual
+        upper[begin:end, :] = dot(back_residual, down, ((1,), (1,)))
+        for t in range(begin, end, sub):
+            gated_back[t : t + sub, :] = (
+                upper[t : t + sub, :] * inner[t : t + sub, :]).astype(BF16)
+    loss = jnp.sum(loss, axis=1, keepdims=True)
 
     def stash(slot, value):
         for l in range(L):
@@ -320,24 +338,14 @@
             out[e * piece : (e + 1) * piece, :] = rec_d[slot, e]
 
     sent = []
-    back_residual = dot(flow, ro[...], ((0,), (0,))).astype(BF16)
-    stash(0, dot(gated[...], back_residual, ((0,), (0,))))
+    stash(0, dot(gated[...], back[...], ((0,), (0,))))
     sent += start_a(0)
-
-    upper[...] = dot(back_residual, down, ((1,), (1,)))
-
-    def back_step(t, carry):
-        span = pl.ds(pl.multiple_of(t * sub, sub), sub)
-        gated[span, :] = (upper[span, :] * inner[span, :]).astype(BF16)
-        return carry
-
-    lax.fori_loop(0, points // sub, back_step, 0)
-    stash(1, dot(gated[...], normed[...], ((0,), (0,))))
+    stash(1, dot(gated_back[...], normed[...], ((0,), (0,))))
     sent += start_a(1)
     sent += start_b(0)
 
-    out_grad = dot(flow, residual, ((1,), (0,)))
-    chunk = SMALL_ROWS // E
+    out_grad = dot(flows[...], resid[...], ((1,), (0,)))
+    chunk = SMALL_ROWS // (2 * E)
 
     def put(row, value):
         done = 0
@@ -350,7 +358,7 @@
 
     put(0, out_grad[:GRAD_ROW])
 
-    upper[:, 0:channels] = dot(gated[...], up, ((1,), (0,)))
+    upper[:, 0:channels] = dot(gated_back[...], up, ((1,), (0,)))
     gain_sum = jnp.zeros((1, channels), F32)
     for i in range(slab):
         back_norm = upper[i * zonal : (i + 1) * zonal, 0:channels]
@@ -364,58 +372,61 @@
         )
     sent += start_b(1)
 
-    lane = 16
-    for b in range(SIDE):
-        def body(t, sums):
-            base = pl.multiple_of(t * lane, lane)
-            sums = list(sums)
-            g = [depth[i, pl.ds(base, lane), :] for i in range(slab)]
+    lane = 32
+
+    def tap_columns(b, carry):
+        sums = [jnp.zeros((8, channels), F32) for _ in range(SIDE)]
+        for base in range(0, zonal, lane):
+            g = [depth[i, base : base + lane, :] for i in range(slab)]
+            wides = [jnp.zeros((lane, channels), F32)] * SIDE
             for r in range(2 * HALF + slab):
                 x = wide[r, pl.ds(base + PAD - HALF + b, lane), :]
                 for i in range(slab):
                     a = r - i
                     if 0 <= a < SIDE:
-                        sums[a] = sums[a] + g[i] * x
-            return tuple(sums)
-
-        sums = lax.fori_loop(
-            0, zonal // lane, body, tuple(jnp.zeros((lane, channels), F32) for _ in range(SIDE))
-        )
+                        wides[a] = wides[a] + g[i] * x
+            for a in range(SIDE):
+                sums[a] = sums[a] + jnp.sum(wides[a].reshape(lane // 8, 8, channels), axis=0)
         for a in range(SIDE):
-            put(GRAD_ROW + a * SIDE + b, jnp.sum(sums[a], axis=0, keepdims=True))
+            tap_grad[pl.ds(a * SIDE + b, 1), :] = jnp.sum(sums[a], axis=0, keepdims=True)
+        return carry
+
+    lax.fori_loop(0, 4, tap_columns, 0)
+    sent += start_c(0)
+    lax.fori_loop(4, SIDE, tap_columns, 0)
+    put(GRAD_ROW, tap_grad[...])
     tail = GRAD_ROW + SIDE * SIDE
     put(tail, gain_sum)
     put(tail + 1, jnp.broadcast_to(loss, (1, channels)))
     put(tail + 2, jnp.zeros((SMALL_ROWS - tail - 2, channels), F32))
 
-    copy = remote(small, small_a, a_send.at[2], a_recv.at[2], at(ens, sibling))
-    copy.start()
-    sent.append(copy)
-    sent += start_c(0)
-    copy.wait_recv()
-    small_pb[...] = small[...] + small_a[...]
-    small_b[pl.ds(ens, 1)] = small_pb[pl.ds(ens, 1)]
-    sent += scatter(lambda e: small_pb.at[e], small_b, b_send.at[2], b_recv.at[2], ens, E, by_ens)
+    plane = ens * 2 + core
+
+    def by_plane(o):
+        return at(o // 2, z * 2 + o % 2)
+
+    small_b[pl.ds(plane, 1)] = small[pl.ds(plane, 1)]
+    sent += scatter(lambda o: small.at[o], small_b, p_send, p_recv, plane, 2 * E, by_plane)
     sent += start_c(1)
     sent += start_d(0)
-    arrive(small_b, b_send.at[2], b_recv.at[2], ens, E, by_ens)
+    arrive(small_b, p_send, p_recv, plane, 2 * E, by_plane)
     total = small_b[0]
-    for e in range(1, E):
-        total = total + small_b[e]
+    for o in range(1, 2 * E):
+        total = total + small_b[o]
     small_pc[...] = total
     small_c[pl.ds(z, 1)] = total[None]
-    sent += scatter(lambda o: small_pc, small_c, c_send.at[2], c_recv.at[2], z, Z, by_z)
+    sent += scatter(lambda o: small_pc, small_c, q_send, q_recv, z, Z, by_z)
     sent += start_d(1)
-    arrive(small_c, c_send.at[2], c_recv.at[2], z, Z, by_z)
+    arrive(small_c, q_send, q_recv, z, Z, by_z)
     total = small_c[0]
     for o in range(1, Z):
         total = total + small_c[o]
-    small_d[pl.ds(ens, 1)] = total[None]
-    sent += scatter(lambda e: small_d.at[ens], small_d, d_send.at[2], d_recv.at[2], ens, E, by_ens)
+    small_d[pl.ds(plane, 1)] = total[None]
+    sent += scatter(lambda o: small_d.at[plane], small_d, r_send, r_recv, plane, 2 * E, by_plane)
     finish(0, down_o)
     finish(1, up_o)
-    arrive(small_d, d_send.at[2], d_recv.at[2], ens, E, by_ens)
-    final = small_d[...].reshape(SMALL_ROWS, channels)
+    arrive(small_d, r_send, r_recv, plane, 2 * E, by_plane)
+    final = jnp.concatenate([small_d[o] for o in range(2 * E)], axis=0)
     out_o[...] = final[:quantities]
     taps_o[...] = final[GRAD_ROW:tail]
     gain_o[...] = final[tail : tail + 1]
@@ -431,6 +442,17 @@
     @pl.when(lat > 0)
     def _():
         north.wait_send()
+
+
+def finish_kernel(*refs):
+    count = (len(refs) - 1) // 2
+    copies = [
+        pltpu.make_async_copy(refs[n], refs[count + n], refs[-1].at[n]) for n in range(count)
+    ]
+    for copy in copies:
+        copy.start()
+    for copy in copies:
+        copy.wait()
 
 
 def on_device(
@@ -446,25 +468,34 @@
     piece = unit // E
     points = slab * zonal
     rows = -(-quantities // 16) * 16
-    chunk = SMALL_ROWS // E
+    chunk = SMALL_ROWS // (2 * E)
     vmem = pl.BlockSpec(memory_space=pltpu.VMEM)
     dma = pltpu.SemaphoreType.DMA
     out = jax.ShapeDtypeStruct
-    crps, taps, gain, up, down, head, look, spread = pl.pallas_call(
+    hbm = pl.BlockSpec(memory_space=pltpu.HBM)
+    grid = (1, quantities, slab, zonal)
+    shapes = [
+        out((1, 1), F32),
+        out((SIDE * SIDE, channels), F32),
+        out((1, channels), F32),
+        out((unit, channels), F32),
+        out((unit, channels), F32),
+        out((quantities, channels), F32),
+        out(grid, BF16),
+        out(grid, F32),
+    ]
+    results = pl.pallas_call(
         functools.partial(kernel, (E, L)),
-        out_shape=[
-            out((1, 1), F32),
-            out((SIDE * SIDE, channels), F32),
-            out((1, channels), F32),
-            out((unit, channels), F32),
-            out((unit, channels), F32),
-            out((quantities, channels), F32),
-            out((quantities, points), BF16),
-            out((quantities, points), F32),
-        ],
-        in_specs=[vmem] * 8,
+        out_shape=shapes,
+        in_specs=[hbm] * 8,
         out_specs=[vmem] * 8,
         scratch_shapes=[
+            pltpu.VMEM((slab, zonal, channels), BF16),
+            pltpu.VMEM((1, slab, zonal, channels), BF16),
+            pltpu.VMEM((quantities, slab, zonal), F32),
+            pltpu.VMEM((SIDE * SIDE, channels), F32),
+            pltpu.VMEM((1, channels), F32),
+            pltpu.VMEM((quantities, channels), BF16),
             pltpu.VMEM((slab + 2 * HALF, zonal, channels), BF16),
             pltpu.VMEM((slab + 2 * HALF, zonal + 2 * PAD, channels), F32),
             pltpu.VMEM((SIDE * SIDE, 8, channels), F32),
@@ -476,8 +507,14 @@
             pltpu.VMEM((points, hidden), F32),
             pltpu.VMEM((points, hidden), BF16),
             pltpu.VMEM((rows, channels), BF16),
-            pltpu.VMEM((E, rows, points), BF16),
+            pltpu.VMEM((slab, E, rows, zonal), BF16),
             pltpu.VMEM((L, 2, unit, channels), BF16),
+            pltpu.VMEM((points, channels), BF16),
+            pltpu.VMEM((rows, points), BF16),
+            pltpu.VMEM((points, channels), BF16),
+            pltpu.VMEM((points, hidden), BF16),
+            pltpu.VMEM((rows, slab, zonal), F32),
+            pltpu.VMEM((SIDE * SIDE, channels), F32),
             pltpu.VMEM((2, 2, E, Z, piece, channels), F32),
             pltpu.VMEM((2, E, Z, piece, channels), F32),
             pltpu.VMEM((2, E, Z, piece, channels), F32),
@@ -485,20 +522,21 @@
             pltpu.VMEM((2, Z, piece, channels), F32),
             pltpu.VMEM((2, Z, piece, channels), F32),
             pltpu.VMEM((2, E, piece, channels), F32),
-            pltpu.VMEM((E, chunk, channels), F32),
-            pltpu.VMEM((E, chunk, channels), F32),
-            pltpu.VMEM((E, chunk, channels), F32),
-            pltpu.VMEM((E, chunk, channels), F32),
+            pltpu.VMEM((2 * E, chunk, channels), F32),
+            pltpu.VMEM((2 * E, chunk, channels), F32),
             pltpu.VMEM((chunk, channels), F32),
             pltpu.VMEM((Z, chunk, channels), F32),
-            pltpu.VMEM((E, chunk, channels), F32),
+            pltpu.VMEM((2 * E, chunk, channels), F32),
+            dma((8,)), dma((2,)), dma((2,)),
+            dma((Z,)), dma((Z,)), dma((L,)),
+            dma((slab, E)), dma((slab, E)),
             dma((2,)), dma((2,)),
-            dma((Z,)), dma((Z,)), dma((L,)),
-            dma((E,)), dma((E,)),
-            dma((3,)), dma((3,)),
-            dma((3, E)), dma((3, E)),
-            dma((3, Z)), dma((3, Z)),
-            dma((3, E)), dma((3, E)),
+            dma((2, E)), dma((2, E)),
+            dma((2, Z)), dma((2, Z)),
+            dma((2, E)), dma((2, E)),
+            dma((2 * E,)), dma((2 * E,)),
+            dma((Z,)), dma((Z,)),
+            dma((2 * E,)), dma((2 * E,)),
         ],
         compiler_params=pltpu.CompilerParams(
             collective_id=0, has_side_effects=True, vmem_limit_bytes=40 * 1024 * 1024
@@ -510,10 +548,16 @@
         features, random_perturbation, observed_truth, stencil_taps,
         affine_factor.reshape(1, channels), widen_matrix, shrink_matrix, readout_matrix,
     )
-    grid = (1, quantities, slab, zonal)
+    anywhere = pl.BlockSpec(memory_space=pl.ANY)
+    crps, taps, gain, up, down, head, look, spread = pl.pallas_call(
+        finish_kernel,
+        out_shape=shapes,
+        in_specs=[anywhere] * 8,
+        out_specs=[hbm] * 8,
+        scratch_shapes=[dma((8,))],
+    )(*results)
     return (
-        crps.reshape(()), taps, gain.reshape(channels), up, down, head,
-        look.reshape(grid), spread.reshape(grid),
+        crps.reshape(()), taps, gain.reshape(channels), up, down, head, look, spread,
     )
 
 

time: 50.5 us -> 60.2 us (1.19)
  Pallas kernels: 37 us -> 48.5 us
  between operations: 2.48 us -> 0.67 us
    pallas_call x1 -> x2, Pallas kernels: 37 us -> 48.5 us  [the longest x1 36.5 us: on_device(): pl.pallas_call(functools.partial(kernel, (E, L)), out_shape=shapes, in_sp...]
    reshape x2 -> x0, local copies, waits for them, and re-layouts: 1.39 us -> none  [the longest x1 0.71 us: on_device(): spread.reshape(grid)]
    unnamed x21 -> x30, local copies, waits for them, and re-layouts: 9.23 us -> 10.5 us
where the time goes in v2:
time: 60.2 us; the launch traced here: 59.7 us
  Pallas kernels  48.5 us (81%)
  local copies, waits for them, and re-layouts  10.5 us (17%)
  between operations  0.67 us (1%)
    pallas_call x1, Pallas kernels, on_device(): pl.pallas_call(functools.partial(kernel, (E, L)), out_shape=shapes, in_sp...  36.5 us
    pallas_call x1, Pallas kernels, on_device(): pl.pallas_call(finish_kernel, out_shape=shapes, in_specs=[anywhere] * 8,...  12 us
    unnamed x30, local copies, waits for them, and re-layouts  10.5 us

profile of v2, /device:TPU:0, one launch (start us, length us, event | category | flops | bytes accessed | tf_op | source)
XLA Modules:
  0.0 59.7 jit_solution(14263909853099150583)
XLA Ops:
  0.6 0.0 copy-start.14
  0.6 0.6 %copy-done.14 = f32[128]{0:T(128)S(1)} copy-done((f32[128]{0:T(128)S(1)}, f32[128]{0:T(128)}, u32[]{:S(2)}) %copy-start.14) | copy-done | bytes 536
  1.3 0.0 copy-start.7
  1.3 0.9 %copy-done.7 = f32[69,4,128]{2,1,0:T(4,128)S(1)} copy-done((f32[69,4,128]{2,1,0:T(4,128)S(1)}, f32[69,4,128]{2,1,0:T(4,128)}, u32[]{:S(2)}) %copy-start.7) | copy-done | bytes 141336
  2.2 0.0 copy-start.8
  2.2 0.9 %copy-done.8 = bf16[4,128,128]{2,1,0:T(8,128)(2,1)S(1)} copy-done((bf16[4,128,128]{2,1,0:T(8,128)(2,1)S(1)}, bf16[4,128,128]{2,1,0:T(8,128)(2,1)}, u32[]{:S(2)}) %copy-start.8) | copy-done | bytes 131096
  3.1 0.0 copy-start.9
  3.1 0.9 %copy-done.9 = bf16[1,4,128,128]{3,2,1,0:T(8,128)(2,1)S(1)} copy-done((bf16[1,4,128,128]{3,2,1,0:T(8,128)(2,1)S(1)}, bf16[1,4,128,128]{3,2,1,0:T(8,128)(2,1)}, u32[]{:S(2)}) %copy-start.9) | copy-done | bytes 131096
  4.0 0.0 copy-start.10
  4.0 0.7 %copy-done.10 = f32[49,128]{1,0:T(8,128)S(1)} copy-done((f32[49,128]{1,0:T(8,128)S(1)}, f32[49,128]{1,0:T(8,128)}, u32[]{:S(2)}) %copy-start.10) | copy-done | bytes 25112
  4.8 0.0 copy-start.11
  4.8 0.7 %copy-done.11 = bf16[69,128]{1,0:T(8,128)(2,1)S(1)} copy-done((bf16[69,128]{1,0:T(8,128)(2,1)S(1)}, bf16[69,128]{1,0:T(8,128)(2,1)}, u32[]{:S(2)}) %copy-start.11) | copy-done | bytes 17688
  5.5 0.0 copy-start.12
  5.5 0.7 %copy-done.12 = bf16[64,128]{1,0:T(8,128)(2,1)S(1)} copy-done((bf16[64,128]{1,0:T(8,128)(2,1)S(1)}, bf16[64,128]{1,0:T(8,128)(2,1)}, u32[]{:S(2)}) %copy-start.12) | copy-done | bytes 16408
  6.2 0.0 copy-start.13
  6.2 0.7 %copy-done.13 = bf16[64,128]{1,0:T(8,128)(2,1)S(1)} copy-done((bf16[64,128]{1,0:T(8,128)(2,1)S(1)}, bf16[64,128]{1,0:T(8,128)(2,1)}, u32[]{:S(2)}) %copy-start.13) | copy-done | bytes 16408
  6.9 36.5 %shard_map.143 = (f32[1,1]{1,0:T(1,128)}, f32[49,128]{1,0:T(8,128)S(1)}, f32[1,128]{1,0:T(1,128)S(1)}, f32[64,128]{1,0:T(8,128)S(1)}, f32[64,128]{1,0:T(8,128)S(...) custom-call(bf16[4,128,128]{2,1,0:T(8,128)(2,1)S(1)} %copy-done.8, ...), custom_call_target="tpu_custom_call" | custom-call | flops 402653184 | bytes 2000000 | tf_op jit(solution)/shard_map/pallas_call | solution.py:487
  43.4 0.0 copy-start
  43.4 0.6 %copy-done = f32[1,69,4,128]{3,2,1,0:T(4,128)} copy-done((f32[1,69,4,128]{3,2,1,0:T(4,128)}, f32[1,69,4,128]{3,2,1,0:T(4,128)S(1)}, u32[]{:S(2)}) %copy-start) | copy-done | bytes 141336
  44.1 0.0 copy-start.1
  44.1 0.6 %copy-done.1 = bf16[1,69,4,128]{3,2,1,0:T(4,128)(2,1)} copy-done((bf16[1,69,4,128]{3,2,1,0:T(4,128)(2,1)}, bf16[1,69,4,128]{3,2,1,0:T(4,128)(2,1)S(1)}, u32[]{:S(2)}) %copy-start.1) | copy-done | bytes 70680
  44.7 0.0 copy-start.2
  44.7 0.6 %copy-done.2 = f32[69,128]{1,0:T(8,128)} copy-done((f32[69,128]{1,0:T(8,128)}, f32[69,128]{1,0:T(8,128)S(1)}, u32[]{:S(2)}) %copy-start.2) | copy-done | bytes 35352
  45.3 0.0 copy-start.3
  45.3 0.6 %copy-done.3 = f32[64,128]{1,0:T(8,128)} copy-done((f32[64,128]{1,0:T(8,128)}, f32[64,128]{1,0:T(8,128)S(1)}, u32[]{:S(2)}) %copy-start.3) | copy-done | bytes 32792
  45.9 0.0 copy-start.4
  45.9 0.6 copy-done.4
  46.5 0.0 copy-start.5
  46.5 0.6 %copy-done.5 = f32[49,128]{1,0:T(8,128)} copy-done((f32[49,128]{1,0:T(8,128)}, f32[49,128]{1,0:T(8,128)S(1)}, u32[]{:S(2)}) %copy-start.5) | copy-done | bytes 25112
  47.1 0.0 copy-start.6
  47.1 0.6 copy-done.6
  47.7 12.0 %shard_map.144 = (f32[1,1]{1,0:T(1,128)}, f32[49,128]{1,0:T(8,128)}, f32[1,128]{1,0:T(1,128)}, f32[64,128]{1,0:T(8,128)}, f32[64,128]{1,0:T(8,128)}, /*index=5*/...) custom-call(f32[1,1]{1,0:T(1,128)} %get-tuple-element.24.refs_0_, f32[49,128]{1,0:T(8,128)} %copy-done.5, ...), custom_call_target="tpu_custom_call" | custom-call | tf_op jit(solution)/shard_map/pallas_call | solution.py:552
Async XLA Ops:
  0.6 0.7 %copy-start.14 = (f32[128]{0:T(128)S(1)}, f32[128]{0:T(128)}, u32[]{:S(2)}) copy-start(f32[128]{0:T(128)} %param.12) | copy-start | bytes 1540
  1.3 0.9 %copy-start.7 = (f32[69,4,128]{2,1,0:T(4,128)S(1)}, f32[69,4,128]{2,1,0:T(4,128)}, u32[]{:S(2)}) copy-start(f32[69,4,128]{2,1,0:T(4,128)} %obs_h.1) | copy-start | bytes 423940
  2.2 0.9 %copy-start.8 = (bf16[4,128,128]{2,1,0:T(8,128)(2,1)S(1)}, bf16[4,128,128]{2,1,0:T(8,128)(2,1)}, u32[]{:S(2)}) copy-start(bf16[4,128,128]{2,1,0:T(8,128)(2,1)} %feat_h.1) | copy-start | bytes 393220
  3.1 0.9 %copy-start.9 = (bf16[1,4,128,128]{3,2,1,0:T(8,128)(2,1)S(1)}, bf16[1,4,128,128]{3,2,1,0:T(8,128)(2,1)}, u32[]{:S(2)}) copy-start(bf16[1,4,128,128]{3,2,1,0:T(8,128)(2,1)} %noise_h.1) | copy-start | bytes 393220
  4.0 0.7 %copy-start.10 = (f32[49,128]{1,0:T(8,128)S(1)}, f32[49,128]{1,0:T(8,128)}, u32[]{:S(2)}) copy-start(f32[49,128]{1,0:T(8,128)} %taps_h.1) | copy-start | bytes 75268
  4.8 0.7 %copy-start.11 = (bf16[69,128]{1,0:T(8,128)(2,1)S(1)}, bf16[69,128]{1,0:T(8,128)(2,1)}, u32[]{:S(2)}) copy-start(bf16[69,128]{1,0:T(8,128)(2,1)} %readout_h.1) | copy-start | bytes 52996
  5.5 0.7 %copy-start.12 = (bf16[64,128]{1,0:T(8,128)(2,1)S(1)}, bf16[64,128]{1,0:T(8,128)(2,1)}, u32[]{:S(2)}) copy-start(bf16[64,128]{1,0:T(8,128)(2,1)} %widen_h.1) | copy-start | bytes 49156
  6.2 0.7 %copy-start.13 = (bf16[64,128]{1,0:T(8,128)(2,1)S(1)}, bf16[64,128]{1,0:T(8,128)(2,1)}, u32[]{:S(2)}) copy-start(bf16[64,128]{1,0:T(8,128)(2,1)} %shrink_h.1) | copy-start | bytes 49156
  43.4 0.7 %copy-start = (f32[1,69,4,128]{3,2,1,0:T(4,128)}, f32[1,69,4,128]{3,2,1,0:T(4,128)S(1)}, u32[]{:S(2)}) copy-start(f32[1,69,4,128]{3,2,1,0:T(4,128)S(1)} %get-tuple-element.31.refs_7_) | copy-start | bytes 423940
  44.1 0.6 %copy-start.1 = (bf16[1,69,4,128]{3,2,1,0:T(4,128)(2,1)}, bf16[1,69,4,128]{3,2,1,0:T(4,128)(2,1)S(1)}, u32[]{:S(2)}) copy-start(bf16[1,69,4,128]{3,2,1,0:T(4,128)(2,1)S(1)} %get-tuple-element.30.refs_6_) | copy-start | bytes 211972
  44.7 0.6 %copy-start.2 = (f32[69,128]{1,0:T(8,128)}, f32[69,128]{1,0:T(8,128)S(1)}, u32[]{:S(2)}) copy-start(f32[69,128]{1,0:T(8,128)S(1)} %get-tuple-element.29.refs_5_) | copy-start | bytes 105988
  45.3 0.6 %copy-start.3 = (f32[64,128]{1,0:T(8,128)}, f32[64,128]{1,0:T(8,128)S(1)}, u32[]{:S(2)}) copy-start(f32[64,128]{1,0:T(8,128)S(1)} %get-tuple-element.27.refs_3_) | copy-start | bytes 98308
  45.9 0.6 %copy-start.4 = (f32[64,128]{1,0:T(8,128)}, f32[64,128]{1,0:T(8,128)S(1)}, u32[]{:S(2)}) copy-start(f32[64,128]{1,0:T(8,128)S(1)} %get-tuple-element.28.refs_4_) | copy-start | bytes 98308
  46.5 0.6 %copy-start.5 = (f32[49,128]{1,0:T(8,128)}, f32[49,128]{1,0:T(8,128)S(1)}, u32[]{:S(2)}) copy-start(f32[49,128]{1,0:T(8,128)S(1)} %get-tuple-element.25.refs_1_) | copy-start | bytes 75268
  47.1 0.6 copy-start.6

commit v3 on v2

--- a/solution.py
+++ b/solution.py
@@ -545,16 +545,21 @@
             flops=12 * points * channels * hidden, bytes_accessed=2_000_000, transcendentals=0
         ),
     )(
-        features, random_perturbation, observed_truth, stencil_taps,
-        affine_factor.reshape(1, channels), widen_matrix, shrink_matrix, readout_matrix,
+        *[
+            pltpu.with_memory_space_constraint(value, pltpu.HBM)
+            for value in (
+                features, random_perturbation, observed_truth, stencil_taps,
+                affine_factor.reshape(1, channels), widen_matrix, shrink_matrix, readout_matrix,
+            )
+        ]
     )
-    anywhere = pl.BlockSpec(memory_space=pl.ANY)
     crps, taps, gain, up, down, head, look, spread = pl.pallas_call(
         finish_kernel,
         out_shape=shapes,
-        in_specs=[anywhere] * 8,
+        in_specs=[vmem] * 8,
         out_specs=[hbm] * 8,
         scratch_shapes=[dma((8,))],
+        compiler_params=pltpu.CompilerParams(vmem_limit_bytes=8 * 1024 * 1024),
     )(*results)
     return (
         crps.reshape(()), taps, gain.reshape(channels), up, down, head, look, spread,

time: 60.2 us -> 38.8 us (0.64)
  Pallas kernels: 48.5 us -> 38 us
  local copies, waits for them, and re-layouts: 10.5 us -> 0 us
    pallas_call x1, Pallas kernels: 12 us -> 1.43 us  [on_device(): pl.pallas_call(finish_kernel, out_shape=shapes, in_specs=[vmem] * 8, out_...]
    unnamed x30 -> x0, local copies, waits for them, and re-layouts: 10.5 us -> none
where the time goes in v3:
time: 38.8 us; the launch traced here: 38.7 us
  Pallas kernels  38 us (98%)
  between operations  0.64 us (2%)
    pallas_call x1, Pallas kernels, on_device(): pl.pallas_call(functools.partial(kernel, (E, L)), out_shape=shapes, in_sp...  36.6 us
    pallas_call x1, Pallas kernels, on_device(): pl.pallas_call(finish_kernel, out_shape=shapes, in_specs=[vmem] * 8, out_...  1.43 us

profile of v3, /device:TPU:0, one launch (start us, length us, event | category | flops | bytes accessed | tf_op | source)
XLA Modules:
  0.0 38.7 jit_solution(9896895826562740039)
XLA Ops:
  0.6 36.6 %shard_map.143 = (f32[1,1]{1,0:T(1,128)}, f32[49,128]{1,0:T(8,128)S(1)}, f32[1,128]{1,0:T(1,128)S(1)}, f32[64,128]{1,0:T(8,128)S(1)}, f32[64,128]{1,0:T(8,128)S(...) custom-call(bf16[4,128,128]{2,1,0:T(8,128)(2,1)} %feat_h.1, ...), custom_call_target="tpu_custom_call" | custom-call | flops 402653184 | bytes 2000000 | tf_op jit(solution)/shard_map/pallas_call | solution.py:487
  37.2 1.4 %shard_map.144 = (f32[1,1]{1,0:T(1,128)}, f32[49,128]{1,0:T(8,128)}, f32[1,128]{1,0:T(1,128)}, f32[64,128]{1,0:T(8,128)}, f32[64,128]{1,0:T(8,128)}, /*index=5*/...) custom-call(f32[1,1]{1,0:T(1,128)} %get-tuple-element.24.refs_0_, ...), custom_call_target="tpu_custom_call" | custom-call | tf_op jit(solution)/shard_map/pallas_call | solution.py:556

commit v4 on v3

--- a/solution.py
+++ b/solution.py
@@ -31,7 +31,7 @@
     crps_o, taps_o, gain_o, up_o, down_o, out_o, look_o, spread_o,
     feat, noise, obs, taps, gain, readout,
     ext, wide, tapb, depth, scaled_s, inv_s, normed, upper, inner, gated, ro, looks, wbuf,
-    resid, flows, back, gated_back, outlook, tap_grad,
+    resid, flows, back, gated_back, outlook, truths, tap_grad,
     grads, rec_a, part_b, rec_b, part_c, rec_c, rec_d,
     small, small_b, small_pc, small_c, small_d,
     in_sem, halo_send, halo_recv, w_send, w_fwd, w_recv, e_send, e_recv,
@@ -87,36 +87,36 @@
         wide[start : start + count, 0:PAD, :] = block[:, zonal - PAD :, :]
         wide[start : start + count, PAD + zonal :, :] = block[:, :PAD, :]
 
-    loads[0].wait()
-    loads[1].wait()
-    field = (feat[...].astype(F32) + noise[0].astype(F32)).astype(BF16)
-    ext[HALF : HALF + slab] = field
     pl.semaphore_wait(barrier, L - 1 + 2 * (E - 1))
-
-    south = remote(ext.at[pl.ds(slab, HALF)], ext.at[pl.ds(0, HALF)],
-                   halo_send.at[0], halo_recv.at[0], at(ens, jnp.minimum(lat + 1, L - 1)))
-    north = remote(ext.at[pl.ds(HALF, HALF)], ext.at[pl.ds(HALF + slab, HALF)],
-                   halo_send.at[1], halo_recv.at[1], at(ens, jnp.maximum(lat - 1, 0)))
-
-    @pl.when(lat < L - 1)
-    def _():
-        south.start()
-
-    @pl.when(lat > 0)
-    def _():
-        north.start()
-
+    loads[2].wait()
+    loads[3].wait()
     own = [
         remote(wbuf.at[lat], wbuf.at[lat], w_send.at[k], w_recv.at[lat],
                at(ens, ((z + k) % Z) * 2 + core))
         for k in range(1, Z)
     ]
-    loads[2].wait()
-    loads[3].wait()
     for copy in own:
         copy.start()
     forwards = [remote(wbuf.at[lat], wbuf.at[lat], w_fwd.at[0], w_recv.at[lat], at(ens, sibling))]
     forwards[0].start()
+
+    loads[0].wait()
+    loads[1].wait()
+    field = (feat[...].astype(F32) + noise[0].astype(F32)).astype(BF16)
+    ext[HALF : HALF + slab] = field
+
+    south = remote(ext.at[pl.ds(slab, HALF)], ext.at[pl.ds(0, HALF)],
+                   halo_send.at[0], halo_recv.at[0], at(ens, jnp.minimum(lat + 1, L - 1)))
+    north = remote(ext.at[pl.ds(HALF, HALF)], ext.at[pl.ds(HALF + slab, HALF)],
+                   halo_send.at[1], halo_recv.at[1], at(ens, jnp.maximum(lat - 1, 0)))
+
+    @pl.when(lat < L - 1)
+    def _():
+        south.start()
+
+    @pl.when(lat > 0)
+    def _():
+        north.start()
 
     widen_rows(HALF, slab)
     for copy in loads[4:]:
@@ -200,8 +200,11 @@
     down = wbuf[:, 1].reshape(hidden, channels)
     sub = 32
     shares = []
-    for i in range(slab):
-        begin, end = i * zonal, (i + 1) * zonal
+    parts = 2 if slab % 2 == 0 else 1
+    span = points // parts
+    lines = slab // parts
+    for i in range(parts):
+        begin, end = i * span, (i + 1) * span
         upper[begin:end, :] = dot(normed[begin:end, :], up, ((1,), (1,)))
         for t in range(begin, end, sub):
             u = upper[t : t + sub, :]
@@ -209,7 +212,8 @@
             inner[t : t + sub, :] = th
             gated[t : t + sub, :] = (0.5 * u * (1.0 + th)).astype(BF16)
         mixed = dot(gated[begin:end, :], down, ((1,), (0,)))
-        residual = (ext[HALF + i].astype(F32) + mixed).astype(BF16)
+        field = ext[HALF + i * lines : HALF + (i + 1) * lines].reshape(span, channels)
+        residual = (field.astype(F32) + mixed).astype(BF16)
         resid[begin:end, :] = residual
         mine = dot(ro[...], residual, ((1,), (1,))).astype(BF16)
         looks[i, pl.ds(ens, 1)] = mine[None]
@@ -218,7 +222,9 @@
                           at((ens + k) % E, lat))
             copy.start()
             shares.append(copy)
-        outlook[:, i, :] = mine.astype(F32)
+        mine = mine.astype(F32)
+        for n in range(lines):
+            outlook[:, i * lines + n, :] = mine[:, n * zonal : (n + 1) * zonal]
 
     look_o[0] = outlook[0:quantities].astype(BF16)
 
@@ -232,22 +238,25 @@
     members = E
     pair_norm = 1.0 / (members * (members - 1))
     latitudes = slab * L
-    loss = jnp.zeros((1, channels), F32)
+    row = lax.broadcasted_iota(jnp.int32, (slab, zonal), 0) + lat * slab
+    area = jnp.cos(math.pi * ((row.astype(F32) + 0.5) / latitudes - 0.5))
+    weights = area * (1.0 / (latitudes * zonal))
+    truths[...] = jnp.zeros_like(truths)
     for i in range(slab):
-        begin, end = i * zonal, (i + 1) * zonal
-        row = jnp.full((8, zonal), lat * slab + i, jnp.int32).astype(F32)
-        area = jnp.cos(math.pi * ((row + 0.5) / latitudes - 0.5))
-        weight = (area * (1.0 / (latitudes * zonal)))[0:1]
+        truths[0:quantities, i * zonal : (i + 1) * zonal] = obs[:, i, :]
+    loss = jnp.zeros((1, span), F32)
+    for i in range(parts):
+        begin, end = i * span, (i + 1) * span
+        weight = jnp.concatenate(
+            [weights[i * lines + n : i * lines + n + 1] for n in range(lines)], axis=1)
         mine = looks[i, pl.ds(ens, 1)][0].astype(F32)
-        truth = jnp.concatenate(
-            [obs[:, i, :], jnp.zeros((rows - quantities, zonal), F32)], axis=0)
-        miss = mine - truth
+        miss = mine - truths[:, begin:end]
         square = miss * miss + SMOOTHING
         root = lax.rsqrt(square)
         miss_size = square * root
         miss_slope = miss * root
-        spread = jnp.full((rows, zonal), math.sqrt(SMOOTHING), F32)
-        ranks = jnp.zeros((rows, zonal), F32)
+        spread = jnp.full((rows, span), math.sqrt(SMOOTHING), F32)
+        ranks = jnp.zeros((rows, span), F32)
         for k in range(1, E):
             other = (ens + k) % E
             remote(looks.at[i, other], looks.at[i, other], e_send.at[i, k], e_recv.at[i, other],
@@ -257,7 +266,7 @@
             root = lax.rsqrt(square)
             spread = spread + square * root
             ranks = ranks + gap * root
-        spread_o[0, :, i, :] = spread[:quantities] * (1.0 / (members - 1))
+        truths[:, begin:end] = spread * (1.0 / (members - 1))
         part = weight * (miss_size / members - 0.5 * pair_norm * spread)
         loss = loss + jnp.sum(part[:quantities], axis=0, keepdims=True)
         flow = (weight * (miss_slope / members - pair_norm * ranks)).astype(BF16)
@@ -274,13 +283,8 @@
         for l in range(L):
             for e in range(E):
                 begin = (l * E + e) * piece
-                grads[slot, l % 2, e, l // 2] = value[begin : begin + piece]
-
-    def start_a(slot):
-        copy = remote(grads.at[slot, 1 - core], rec_a.at[slot], a_send.at[slot], a_recv.at[slot],
-                      at(ens, sibling))
-        copy.start()
-        return [copy]
+                grads[l % 2, e, l // 2, slot * piece : (slot + 1) * piece] = (
+                    value[begin : begin + piece])
 
     def scatter(src, dst, send, recv, me, count, place):
         copies = [
@@ -304,45 +308,10 @@
     def by_z(other):
         return at(ens, other * 2 + core)
 
-    def start_b(slot):
-        sent = remote(grads.at[slot, 1 - core], rec_a.at[slot], a_send.at[slot], a_recv.at[slot],
-                      at(ens, sibling))
-        sent.wait_recv()
-        part_b[slot] = grads[slot, pl.ds(core, 1)][0] + rec_a[slot]
-        rec_b[slot, pl.ds(ens, 1)] = part_b[slot, pl.ds(ens, 1)]
-        return scatter(lambda e: part_b.at[slot, e], rec_b.at[slot], b_send.at[slot],
-                       b_recv.at[slot], ens, E, by_ens)
-
-    def start_c(slot):
-        arrive(rec_b.at[slot], b_send.at[slot], b_recv.at[slot], ens, E, by_ens)
-        total = rec_b[slot, 0]
-        for e in range(1, E):
-            total = total + rec_b[slot, e]
-        part_c[slot] = total
-        rec_c[slot, pl.ds(z, 1)] = part_c[slot, pl.ds(z, 1)]
-        return scatter(lambda o: part_c.at[slot, o], rec_c.at[slot], c_send.at[slot],
-                       c_recv.at[slot], z, Z, by_z)
-
-    def start_d(slot):
-        arrive(rec_c.at[slot], c_send.at[slot], c_recv.at[slot], z, Z, by_z)
-        total = rec_c[slot, 0]
-        for o in range(1, Z):
-            total = total + rec_c[slot, o]
-        rec_d[slot, pl.ds(ens, 1)] = total[None]
-        return scatter(lambda e: rec_d.at[slot, ens], rec_d.at[slot], d_send.at[slot],
-                       d_recv.at[slot], ens, E, by_ens)
-
-    def finish(slot, out):
-        arrive(rec_d.at[slot], d_send.at[slot], d_recv.at[slot], ens, E, by_ens)
-        for e in range(E):
-            out[e * piece : (e + 1) * piece, :] = rec_d[slot, e]
-
-    sent = []
     stash(0, dot(gated[...], back[...], ((0,), (0,))))
-    sent += start_a(0)
     stash(1, dot(gated_back[...], normed[...], ((0,), (0,))))
-    sent += start_a(1)
-    sent += start_b(0)
+    halves = remote(grads.at[1 - core], rec_a, a_send.at[0], a_recv.at[0], at(ens, sibling))
+    halves.start()
 
     out_grad = dot(flows[...], resid[...], ((1,), (0,)))
     chunk = SMALL_ROWS // (2 * E)
@@ -370,7 +339,10 @@
             - jnp.mean(g, axis=-1, keepdims=True)
             - scaled * jnp.mean(g * scaled, axis=-1, keepdims=True)
         )
-    sent += start_b(1)
+    halves.wait_recv()
+    part_b[...] = grads[pl.ds(core, 1)][0] + rec_a[...]
+    rec_b[pl.ds(ens, 1)] = part_b[pl.ds(ens, 1)]
+    sent_b = scatter(lambda e: part_b.at[e], rec_b, b_send, b_recv, ens, E, by_ens)
 
     lane = 32
 
@@ -392,7 +364,13 @@
         return carry
 
     lax.fori_loop(0, 4, tap_columns, 0)
-    sent += start_c(0)
+    arrive(rec_b, b_send, b_recv, ens, E, by_ens)
+    total = rec_b[0]
+    for e in range(1, E):
+        total = total + rec_b[e]
+    part_c[...] = total
+    rec_c[pl.ds(z, 1)] = part_c[pl.ds(z, 1)]
+    sent_c = scatter(lambda o: part_c.at[o], rec_c, c_send, c_recv, z, Z, by_z)
     lax.fori_loop(4, SIDE, tap_columns, 0)
     put(GRAD_ROW, tap_grad[...])
     tail = GRAD_ROW + SIDE * SIDE
@@ -406,25 +384,46 @@
         return at(o // 2, z * 2 + o % 2)
 
     small_b[pl.ds(plane, 1)] = small[pl.ds(plane, 1)]
-    sent += scatter(lambda o: small.at[o], small_b, p_send, p_recv, plane, 2 * E, by_plane)
-    sent += start_c(1)
-    sent += start_d(0)
+    sent_p = scatter(lambda o: small.at[o], small_b, p_send, p_recv, plane, 2 * E, by_plane)
+    arrive(rec_c, c_send, c_recv, z, Z, by_z)
+    total = rec_c[0]
+    for o in range(1, Z):
+        total = total + rec_c[o]
+    rec_d[pl.ds(ens, 1)] = total[None]
+    sent_d = scatter(lambda e: rec_d.at[ens], rec_d, d_send, d_recv, ens, E, by_ens)
     arrive(small_b, p_send, p_recv, plane, 2 * E, by_plane)
     total = small_b[0]
     for o in range(1, 2 * E):
         total = total + small_b[o]
     small_pc[...] = total
     small_c[pl.ds(z, 1)] = total[None]
-    sent += scatter(lambda o: small_pc, small_c, q_send, q_recv, z, Z, by_z)
-    sent += start_d(1)
+    sent_q = scatter(lambda o: small_pc, small_c, q_send, q_recv, z, Z, by_z)
+
+    for i in range(slab):
+        spread_o[0, :, i, :] = truths[0:quantities, i * zonal : (i + 1) * zonal]
+    for copy in own + forwards + shares + [halves] + sent_b:
+        copy.wait_send()
+
+    @pl.when(lat < L - 1)
+    def _():
+        south.wait_send()
+
+    @pl.when(lat > 0)
+    def _():
+        north.wait_send()
+
     arrive(small_c, q_send, q_recv, z, Z, by_z)
     total = small_c[0]
     for o in range(1, Z):
         total = total + small_c[o]
     small_d[pl.ds(plane, 1)] = total[None]
-    sent += scatter(lambda o: small_d.at[plane], small_d, r_send, r_recv, plane, 2 * E, by_plane)
-    finish(0, down_o)
-    finish(1, up_o)
+    sent_r = scatter(lambda o: small_d.at[plane], small_d, r_send, r_recv, plane, 2 * E, by_plane)
+    arrive(rec_d, d_send, d_recv, ens, E, by_ens)
+    for e in range(E):
+        down_o[e * piece : (e + 1) * piece, :] = rec_d[e, 0:piece]
+        up_o[e * piece : (e + 1) * piece, :] = rec_d[e, piece : 2 * piece]
+    for copy in sent_c + sent_p + sent_d + sent_q:
+        copy.wait_send()
     arrive(small_d, r_send, r_recv, plane, 2 * E, by_plane)
     final = jnp.concatenate([small_d[o] for o in range(2 * E)], axis=0)
     out_o[...] = final[:quantities]
@@ -432,16 +431,8 @@
     gain_o[...] = final[tail : tail + 1]
     crps_o[...] = final[tail + 1 : tail + 2, 0:1]
 
-    for copy in own + forwards + shares + sent:
+    for copy in sent_r:
         copy.wait_send()
-
-    @pl.when(lat < L - 1)
-    def _():
-        south.wait_send()
-
-    @pl.when(lat > 0)
-    def _():
-        north.wait_send()
 
 
 def finish_kernel(*refs):
@@ -467,6 +458,7 @@
     hidden = unit * L
     piece = unit // E
     points = slab * zonal
+    parts = 2 if slab % 2 == 0 else 1
     rows = -(-quantities // 16) * 16
     chunk = SMALL_ROWS // (2 * E)
     vmem = pl.BlockSpec(memory_space=pltpu.VMEM)
@@ -507,21 +499,22 @@
             pltpu.VMEM((points, hidden), F32),
             pltpu.VMEM((points, hidden), BF16),
             pltpu.VMEM((rows, channels), BF16),
-            pltpu.VMEM((slab, E, rows, zonal), BF16),
+            pltpu.VMEM((parts, E, rows, points // parts), BF16),
             pltpu.VMEM((L, 2, unit, channels), BF16),
             pltpu.VMEM((points, channels), BF16),
             pltpu.VMEM((rows, points), BF16),
             pltpu.VMEM((points, channels), BF16),
             pltpu.VMEM((points, hidden), BF16),
             pltpu.VMEM((rows, slab, zonal), F32),
+            pltpu.VMEM((rows, points), F32),
             pltpu.VMEM((SIDE * SIDE, channels), F32),
-            pltpu.VMEM((2, 2, E, Z, piece, channels), F32),
-            pltpu.VMEM((2, E, Z, piece, channels), F32),
-            pltpu.VMEM((2, E, Z, piece, channels), F32),
-            pltpu.VMEM((2, E, Z, piece, channels), F32),
-            pltpu.VMEM((2, Z, piece, channels), F32),
-            pltpu.VMEM((2, Z, piece, channels), F32),
-            pltpu.VMEM((2, E, piece, channels), F32),
+            pltpu.VMEM((2, E, Z, 2 * piece, channels), F32),
+            pltpu.VMEM((E, Z, 2 * piece, channels), F32),
+            pltpu.VMEM((E, Z, 2 * piece, channels), F32),
+            pltpu.VMEM((E, Z, 2 * piece, channels), F32),
+            pltpu.VMEM((Z, 2 * piece, channels), F32),
+            pltpu.VMEM((Z, 2 * piece, channels), F32),
+            pltpu.VMEM((E, 2 * piece, channels), F32),
             pltpu.VMEM((2 * E, chunk, channels), F32),
             pltpu.VMEM((2 * E, chunk, channels), F32),
             pltpu.VMEM((chunk, channels), F32),
@@ -530,10 +523,10 @@
             dma((8,)), dma((2,)), dma((2,)),
             dma((Z,)), dma((Z,)), dma((L,)),
             dma((slab, E)), dma((slab, E)),
-            dma((2,)), dma((2,)),
-            dma((2, E)), dma((2, E)),
-            dma((2, Z)), dma((2, Z)),
-            dma((2, E)), dma((2, E)),
+            dma((1,)), dma((1,)),
+            dma((E,)), dma((E,)),
+            dma((Z,)), dma((Z,)),
+            dma((E,)), dma((E,)),
             dma((2 * E,)), dma((2 * E,)),
             dma((Z,)), dma((Z,)),
             dma((2 * E,)), dma((2 * E,)),

time: 38.8 us -> 40.5 us (1.044)
  Pallas kernels: 38 us -> 39.7 us
    pallas_call x1, Pallas kernels: 36.6 us -> 38.3 us  [on_device(): pl.pallas_call(functools.partial(kernel, (E, L)), out_shape=shapes, in_sp...]
where the time goes in v4:
time: 40.5 us; the launch traced here: 40.4 us
  Pallas kernels  39.7 us (98%)
  between operations  0.64 us (2%)
    pallas_call x1, Pallas kernels, on_device(): pl.pallas_call(functools.partial(kernel, (E, L)), out_shape=shapes, in_sp...  38.3 us
    pallas_call x1, Pallas kernels, on_device(): pl.pallas_call(finish_kernel, out_shape=shapes, in_specs=[vmem] * 8, out_...  1.43 us

profile of v4, /device:TPU:0, one launch (start us, length us, event | category | flops | bytes accessed | tf_op | source)
XLA Modules:
  0.0 40.4 jit_solution(9453463410730704884)
XLA Ops:
  0.6 38.3 %shard_map.143 = (f32[1,1]{1,0:T(1,128)}, f32[49,128]{1,0:T(8,128)S(1)}, f32[1,128]{1,0:T(1,128)S(1)}, f32[64,128]{1,0:T(8,128)S(1)}, f32[64,128]{1,0:T(8,128)S(...) custom-call(bf16[4,128,128]{2,1,0:T(8,128)(2,1)} %feat_h.1, ...), custom_call_target="tpu_custom_call" | custom-call | flops 402653184 | bytes 2000000 | tf_op jit(solution)/shard_map/pallas_call | solution.py:479
  38.9 1.4 %shard_map.144 = (f32[1,1]{1,0:T(1,128)}, f32[49,128]{1,0:T(8,128)}, f32[1,128]{1,0:T(1,128)}, f32[64,128]{1,0:T(8,128)}, f32[64,128]{1,0:T(8,128)}, /*index=5*/...) custom-call(f32[1,1]{1,0:T(1,128)} %get-tuple-element.24.refs_0_, ...), custom_call_target="tpu_custom_call" | custom-call | tf_op jit(solution)/shard_map/pallas_call | solution.py:549

commit v5 on v4

--- a/solution.py
+++ b/solution.py
@@ -87,7 +87,25 @@
         wide[start : start + count, 0:PAD, :] = block[:, zonal - PAD :, :]
         wide[start : start + count, PAD + zonal :, :] = block[:, :PAD, :]
 
+    loads[0].wait()
+    loads[1].wait()
+    field = (feat[...].astype(F32) + noise[0].astype(F32)).astype(BF16)
+    ext[HALF : HALF + slab] = field
     pl.semaphore_wait(barrier, L - 1 + 2 * (E - 1))
+
+    south = remote(ext.at[pl.ds(slab, HALF)], ext.at[pl.ds(0, HALF)],
+                   halo_send.at[0], halo_recv.at[0], at(ens, jnp.minimum(lat + 1, L - 1)))
+    north = remote(ext.at[pl.ds(HALF, HALF)], ext.at[pl.ds(HALF + slab, HALF)],
+                   halo_send.at[1], halo_recv.at[1], at(ens, jnp.maximum(lat - 1, 0)))
+
+    @pl.when(lat < L - 1)
+    def _():
+        south.start()
+
+    @pl.when(lat > 0)
+    def _():
+        north.start()
+
     loads[2].wait()
     loads[3].wait()
     own = [
@@ -99,24 +117,6 @@
         copy.start()
     forwards = [remote(wbuf.at[lat], wbuf.at[lat], w_fwd.at[0], w_recv.at[lat], at(ens, sibling))]
     forwards[0].start()
-
-    loads[0].wait()
-    loads[1].wait()
-    field = (feat[...].astype(F32) + noise[0].astype(F32)).astype(BF16)
-    ext[HALF : HALF + slab] = field
-
-    south = remote(ext.at[pl.ds(slab, HALF)], ext.at[pl.ds(0, HALF)],
-                   halo_send.at[0], halo_recv.at[0], at(ens, jnp.minimum(lat + 1, L - 1)))
-    north = remote(ext.at[pl.ds(HALF, HALF)], ext.at[pl.ds(HALF + slab, HALF)],
-                   halo_send.at[1], halo_recv.at[1], at(ens, jnp.maximum(lat - 1, 0)))
-
-    @pl.when(lat < L - 1)
-    def _():
-        south.start()
-
-    @pl.when(lat > 0)
-    def _():
-        north.start()
 
     widen_rows(HALF, slab)
     for copy in loads[4:]:
@@ -200,7 +200,7 @@
     down = wbuf[:, 1].reshape(hidden, channels)
     sub = 32
     shares = []
-    parts = 2 if slab % 2 == 0 else 1
+    parts = slab
     span = points // parts
     lines = slab // parts
     for i in range(parts):
@@ -363,7 +363,20 @@
             tap_grad[pl.ds(a * SIDE + b, 1), :] = jnp.sum(sums[a], axis=0, keepdims=True)
         return carry
 
-    lax.fori_loop(0, 4, tap_columns, 0)
+    lax.fori_loop(0, SIDE, tap_columns, 0)
+    put(GRAD_ROW, tap_grad[...])
+    tail = GRAD_ROW + SIDE * SIDE
+    put(tail, gain_sum)
+    put(tail + 1, jnp.broadcast_to(loss, (1, channels)))
+    put(tail + 2, jnp.zeros((SMALL_ROWS - tail - 2, channels), F32))
+
+    plane = ens * 2 + core
+
+    def by_plane(o):
+        return at(o // 2, z * 2 + o % 2)
+
+    small_b[pl.ds(plane, 1)] = small[pl.ds(plane, 1)]
+    sent_p = scatter(lambda o: small.at[o], small_b, p_send, p_recv, plane, 2 * E, by_plane)
     arrive(rec_b, b_send, b_recv, ens, E, by_ens)
     total = rec_b[0]
     for e in range(1, E):
@@ -371,26 +384,6 @@
     part_c[...] = total
     rec_c[pl.ds(z, 1)] = part_c[pl.ds(z, 1)]
     sent_c = scatter(lambda o: part_c.at[o], rec_c, c_send, c_recv, z, Z, by_z)
-    lax.fori_loop(4, SIDE, tap_columns, 0)
-    put(GRAD_ROW, tap_grad[...])
-    tail = GRAD_ROW + SIDE * SIDE
-    put(tail, gain_sum)
-    put(tail + 1, jnp.broadcast_to(loss, (1, channels)))
-    put(tail + 2, jnp.zeros((SMALL_ROWS - tail - 2, channels), F32))
-
-    plane = ens * 2 + core
-
-    def by_plane(o):
-        return at(o // 2, z * 2 + o % 2)
-
-    small_b[pl.ds(plane, 1)] = small[pl.ds(plane, 1)]
-    sent_p = scatter(lambda o: small.at[o], small_b, p_send, p_recv, plane, 2 * E, by_plane)
-    arrive(rec_c, c_send, c_recv, z, Z, by_z)
-    total = rec_c[0]
-    for o in range(1, Z):
-        total = total + rec_c[o]
-    rec_d[pl.ds(ens, 1)] = total[None]
-    sent_d = scatter(lambda e: rec_d.at[ens], rec_d, d_send, d_recv, ens, E, by_ens)
     arrive(small_b, p_send, p_recv, plane, 2 * E, by_plane)
     total = small_b[0]
     for o in range(1, 2 * E):
@@ -412,6 +405,12 @@
     def _():
         north.wait_send()
 
+    arrive(rec_c, c_send, c_recv, z, Z, by_z)
+    total = rec_c[0]
+    for o in range(1, Z):
+        total = total + rec_c[o]
+    rec_d[pl.ds(ens, 1)] = total[None]
+    sent_d = scatter(lambda e: rec_d.at[ens], rec_d, d_send, d_recv, ens, E, by_ens)
     arrive(small_c, q_send, q_recv, z, Z, by_z)
     total = small_c[0]
     for o in range(1, Z):
@@ -458,7 +457,7 @@
     hidden = unit * L
     piece = unit // E
     points = slab * zonal
-    parts = 2 if slab % 2 == 0 else 1
+    parts = slab
     rows = -(-quantities // 16) * 16
     chunk = SMALL_ROWS // (2 * E)
     vmem = pl.BlockSpec(memory_space=pltpu.VMEM)

time: 40.5 us -> 37.8 us (0.933)
  Pallas kernels: 39.7 us -> 37 us
    pallas_call x1, Pallas kernels: 38.3 us -> 35.5 us  [on_device(): pl.pallas_call(functools.partial(kernel, (E, L)), out_shape=shapes, in_sp...]
where the time goes in v5:
time: 37.8 us; the launch traced here: 37.6 us
  Pallas kernels  37 us (98%)
  between operations  0.64 us (2%)
    pallas_call x1, Pallas kernels, on_device(): pl.pallas_call(functools.partial(kernel, (E, L)), out_shape=shapes, in_sp...  35.5 us
    pallas_call x1, Pallas kernels, on_device(): pl.pallas_call(finish_kernel, out_shape=shapes, in_specs=[vmem] * 8, out_...  1.43 us

profile of v5, /device:TPU:0, one launch (start us, length us, event | category | flops | bytes accessed | tf_op | source)
XLA Modules:
  0.0 37.6 jit_solution(11427539914153620847)
XLA Ops:
  0.6 35.5 %shard_map.143 = (f32[1,1]{1,0:T(1,128)}, f32[49,128]{1,0:T(8,128)S(1)}, f32[1,128]{1,0:T(1,128)S(1)}, f32[64,128]{1,0:T(8,128)S(1)}, f32[64,128]{1,0:T(8,128)S(...) custom-call(bf16[4,128,128]{2,1,0:T(8,128)(2,1)} %feat_h.1, ...), custom_call_target="tpu_custom_call" | custom-call | flops 402653184 | bytes 2000000 | tf_op jit(solution)/shard_map/pallas_call | solution.py:478
  36.2 1.4 %shard_map.144 = (f32[1,1]{1,0:T(1,128)}, f32[49,128]{1,0:T(8,128)}, f32[1,128]{1,0:T(1,128)}, f32[64,128]{1,0:T(8,128)}, f32[64,128]{1,0:T(8,128)}, /*index=5*/...) custom-call(f32[1,1]{1,0:T(1,128)} %get-tuple-element.24.refs_0_, ...), custom_call_target="tpu_custom_call" | custom-call | tf_op jit(solution)/shard_map/pallas_call | solution.py:548

commit v6 on v5

--- a/solution.py
+++ b/solution.py
@@ -153,6 +153,14 @@
 
     convolve(range(HALF, HALF + slab), True)
 
+    latitudes = slab * L
+    row = lax.broadcasted_iota(jnp.int32, (slab, zonal), 0) + lat * slab
+    area = jnp.cos(math.pi * ((row.astype(F32) + 0.5) / latitudes - 0.5))
+    weights = area * (1.0 / (latitudes * zonal))
+    truths[...] = jnp.zeros_like(truths)
+    for i in range(slab):
+        truths[0:quantities, i * zonal : (i + 1) * zonal] = obs[:, i, :]
+
     for k in range(1, Z):
         other = ((z + k) % Z) * 2 + core
         remote(wbuf.at[other], wbuf.at[other], w_send.at[k], w_recv.at[other],
@@ -203,14 +211,19 @@
     parts = slab
     span = points // parts
     lines = slab // parts
-    for i in range(parts):
-        begin, end = i * span, (i + 1) * span
-        upper[begin:end, :] = dot(normed[begin:end, :], up, ((1,), (1,)))
-        for t in range(begin, end, sub):
+    def activate(i):
+        for t in range(i * span, (i + 1) * span, sub):
             u = upper[t : t + sub, :]
             th = jnp.tanh(SQRT_TWO_PI * (u + CUBIC * u * u * u))
             inner[t : t + sub, :] = th
             gated[t : t + sub, :] = (0.5 * u * (1.0 + th)).astype(BF16)
+
+    upper[...] = dot(normed[...], up, ((1,), (1,)))
+    activate(0)
+    for i in range(parts):
+        begin, end = i * span, (i + 1) * span
+        if i + 1 < parts:
+            activate(i + 1)
         mixed = dot(gated[begin:end, :], down, ((1,), (0,)))
         field = ext[HALF + i * lines : HALF + (i + 1) * lines].reshape(span, channels)
         residual = (field.astype(F32) + mixed).astype(BF16)
@@ -222,11 +235,7 @@
                           at((ens + k) % E, lat))
             copy.start()
             shares.append(copy)
-        mine = mine.astype(F32)
-        for n in range(lines):
-            outlook[:, i * lines + n, :] = mine[:, n * zonal : (n + 1) * zonal]
-
-    look_o[0] = outlook[0:quantities].astype(BF16)
+
 
     for t in range(0, points, sub):
         u = upper[t : t + sub, :]
@@ -237,13 +246,15 @@
 
     members = E
     pair_norm = 1.0 / (members * (members - 1))
-    latitudes = slab * L
-    row = lax.broadcasted_iota(jnp.int32, (slab, zonal), 0) + lat * slab
-    area = jnp.cos(math.pi * ((row.astype(F32) + 0.5) / latitudes - 0.5))
-    weights = area * (1.0 / (latitudes * zonal))
-    truths[...] = jnp.zeros_like(truths)
-    for i in range(slab):
-        truths[0:quantities, i * zonal : (i + 1) * zonal] = obs[:, i, :]
+    def descend(i):
+        begin, end = i * span, (i + 1) * span
+        back_residual = dot(flows[:, begin:end], ro[...], ((0,), (0,))).astype(BF16)
+        back[begin:end, :] = back_residual
+        upper[begin:end, :] = dot(back_residual, down, ((1,), (1,)))
+        for t in range(begin, end, sub):
+            gated_back[t : t + sub, :] = (
+                upper[t : t + sub, :] * inner[t : t + sub, :]).astype(BF16)
+
     loss = jnp.zeros((1, span), F32)
     for i in range(parts):
         begin, end = i * span, (i + 1) * span
@@ -271,12 +282,9 @@
         loss = loss + jnp.sum(part[:quantities], axis=0, keepdims=True)
         flow = (weight * (miss_slope / members - pair_norm * ranks)).astype(BF16)
         flows[:, begin:end] = flow
-        back_residual = dot(flow, ro[...], ((0,), (0,))).astype(BF16)
-        back[begin:end, :] = back_residual
-        upper[begin:end, :] = dot(back_residual, down, ((1,), (1,)))
-        for t in range(begin, end, sub):
-            gated_back[t : t + sub, :] = (
-                upper[t : t + sub, :] * inner[t : t + sub, :]).astype(BF16)
+        if i > 0:
+            descend(i - 1)
+    descend(parts - 1)
     loss = jnp.sum(loss, axis=1, keepdims=True)
 
     def stash(slot, value):
@@ -330,6 +338,11 @@
     upper[:, 0:channels] = dot(gated_back[...], up, ((1,), (0,)))
     gain_sum = jnp.zeros((1, channels), F32)
     for i in range(slab):
+        if i == slab // 2:
+            halves.wait_recv()
+            part_b[...] = grads[pl.ds(core, 1)][0] + rec_a[...]
+            rec_b[pl.ds(ens, 1)] = part_b[pl.ds(ens, 1)]
+            sent_b = scatter(lambda e: part_b.at[e], rec_b, b_send, b_recv, ens, E, by_ens)
         back_norm = upper[i * zonal : (i + 1) * zonal, 0:channels]
         scaled = scaled_s[i]
         gain_sum = gain_sum + jnp.sum(back_norm * scaled, axis=0, keepdims=True)
@@ -339,11 +352,6 @@
             - jnp.mean(g, axis=-1, keepdims=True)
             - scaled * jnp.mean(g * scaled, axis=-1, keepdims=True)
         )
-    halves.wait_recv()
-    part_b[...] = grads[pl.ds(core, 1)][0] + rec_a[...]
-    rec_b[pl.ds(ens, 1)] = part_b[pl.ds(ens, 1)]
-    sent_b = scatter(lambda e: part_b.at[e], rec_b, b_send, b_recv, ens, E, by_ens)
-
     lane = 32
 
     def tap_columns(b, carry):
@@ -377,6 +385,11 @@
 
     small_b[pl.ds(plane, 1)] = small[pl.ds(plane, 1)]
     sent_p = scatter(lambda o: small.at[o], small_b, p_send, p_recv, plane, 2 * E, by_plane)
+    for i in range(slab):
+        begin = i % lines * zonal
+        mine = looks[i // lines, pl.ds(ens, 1)][0].astype(F32)
+        outlook[:, i, :] = mine[:, begin : begin + zonal]
+    look_o[0] = outlook[0:quantities].astype(BF16)
     arrive(rec_b, b_send, b_recv, ens, E, by_ens)
     total = rec_b[0]
     for e in range(1, E):

time: 37.8 us -> 37.9 us (level)
  no operation moved by 1% of the time
where the time goes in v6:
time: 37.9 us; the launch traced here: 37.7 us
  Pallas kernels  37.1 us (98%)
  between operations  0.64 us (2%)
    pallas_call x1, Pallas kernels, on_device(): pl.pallas_call(functools.partial(kernel, (E, L)), out_shape=shapes, in_sp...  35.6 us
    pallas_call x1, Pallas kernels, on_device(): pl.pallas_call(finish_kernel, out_shape=shapes, in_specs=[vmem] * 8, out_...  1.43 us

profile of v6, /device:TPU:0, one launch (start us, length us, event | category | flops | bytes accessed | tf_op | source)
XLA Modules:
  0.0 37.7 jit_solution(12063463517257354963)
XLA Ops:
  0.6 35.6 %shard_map.143 = (f32[1,1]{1,0:T(1,128)}, f32[49,128]{1,0:T(8,128)S(1)}, f32[1,128]{1,0:T(1,128)S(1)}, f32[64,128]{1,0:T(8,128)S(1)}, f32[64,128]{1,0:T(8,128)S(...) custom-call(bf16[4,128,128]{2,1,0:T(8,128)(2,1)} %feat_h.1, ...), custom_call_target="tpu_custom_call" | custom-call | flops 402653184 | bytes 2000000 | tf_op jit(solution)/shard_map/pallas_call | solution.py:491
  36.3 1.4 %shard_map.144 = (f32[1,1]{1,0:T(1,128)}, f32[49,128]{1,0:T(8,128)}, f32[1,128]{1,0:T(1,128)}, f32[64,128]{1,0:T(8,128)}, f32[64,128]{1,0:T(8,128)}, /*index=5*/...) custom-call(f32[1,1]{1,0:T(1,128)} %get-tuple-element.24.refs_0_, ...), custom_call_target="tpu_custom_call" | custom-call | tf_op jit(solution)/shard_map/pallas_call | solution.py:561

commit v7 on v6

--- a/solution.py
+++ b/solution.py
@@ -87,25 +87,7 @@
         wide[start : start + count, 0:PAD, :] = block[:, zonal - PAD :, :]
         wide[start : start + count, PAD + zonal :, :] = block[:, :PAD, :]
 
-    loads[0].wait()
-    loads[1].wait()
-    field = (feat[...].astype(F32) + noise[0].astype(F32)).astype(BF16)
-    ext[HALF : HALF + slab] = field
     pl.semaphore_wait(barrier, L - 1 + 2 * (E - 1))
-
-    south = remote(ext.at[pl.ds(slab, HALF)], ext.at[pl.ds(0, HALF)],
-                   halo_send.at[0], halo_recv.at[0], at(ens, jnp.minimum(lat + 1, L - 1)))
-    north = remote(ext.at[pl.ds(HALF, HALF)], ext.at[pl.ds(HALF + slab, HALF)],
-                   halo_send.at[1], halo_recv.at[1], at(ens, jnp.maximum(lat - 1, 0)))
-
-    @pl.when(lat < L - 1)
-    def _():
-        south.start()
-
-    @pl.when(lat > 0)
-    def _():
-        north.start()
-
     loads[2].wait()
     loads[3].wait()
     own = [
@@ -117,6 +99,24 @@
         copy.start()
     forwards = [remote(wbuf.at[lat], wbuf.at[lat], w_fwd.at[0], w_recv.at[lat], at(ens, sibling))]
     forwards[0].start()
+
+    loads[0].wait()
+    loads[1].wait()
+    field = (feat[...].astype(F32) + noise[0].astype(F32)).astype(BF16)
+    ext[HALF : HALF + slab] = field
+
+    south = remote(ext.at[pl.ds(slab, HALF)], ext.at[pl.ds(0, HALF)],
+                   halo_send.at[0], halo_recv.at[0], at(ens, jnp.minimum(lat + 1, L - 1)))
+    north = remote(ext.at[pl.ds(HALF, HALF)], ext.at[pl.ds(HALF + slab, HALF)],
+                   halo_send.at[1], halo_recv.at[1], at(ens, jnp.maximum(lat - 1, 0)))
+
+    @pl.when(lat < L - 1)
+    def _():
+        south.start()
+
+    @pl.when(lat > 0)
+    def _():
+        north.start()
 
     widen_rows(HALF, slab)
     for copy in loads[4:]:

time: 37.9 us -> 37.8 us (level)
  no operation moved by 1% of the time
where the time goes in v7:
time: 37.8 us; the launch traced here: 37.6 us
  Pallas kernels  37 us (98%)
  between operations  0.64 us (2%)
    pallas_call x1, Pallas kernels, on_device(): pl.pallas_call(functools.partial(kernel, (E, L)), out_shape=shapes, in_sp...  35.5 us
    pallas_call x1, Pallas kernels, on_device(): pl.pallas_call(finish_kernel, out_shape=shapes, in_specs=[vmem] * 8, out_...  1.43 us

profile of v7, /device:TPU:0, one launch (start us, length us, event | category | flops | bytes accessed | tf_op | source)
XLA Modules:
  0.0 37.6 jit_solution(16251915441419285320)
XLA Ops:
  0.6 35.5 %shard_map.143 = (f32[1,1]{1,0:T(1,128)}, f32[49,128]{1,0:T(8,128)S(1)}, f32[1,128]{1,0:T(1,128)S(1)}, f32[64,128]{1,0:T(8,128)S(1)}, f32[64,128]{1,0:T(8,128)S(...) custom-call(bf16[4,128,128]{2,1,0:T(8,128)(2,1)} %feat_h.1, ...), custom_call_target="tpu_custom_call" | custom-call | flops 402653184 | bytes 2000000 | tf_op jit(solution)/shard_map/pallas_call | solution.py:491
  36.2 1.4 %shard_map.144 = (f32[1,1]{1,0:T(1,128)}, f32[49,128]{1,0:T(8,128)}, f32[1,128]{1,0:T(1,128)}, f32[64,128]{1,0:T(8,128)}, f32[64,128]{1,0:T(8,128)}, /*index=5*/...) custom-call(f32[1,1]{1,0:T(1,128)} %get-tuple-element.24.refs_0_, ...), custom_call_target="tpu_custom_call" | custom-call | tf_op jit(solution)/shard_map/pallas_call | solution.py:561
